TPU v7x, 32 devices: a whole 2x2x4 slice. The times are simulated.
32 devices in a mesh: row: 4 (over y, x), col: 8 (over z, core).
Axes of the slice: x: 2, y: 2, z: 4, core: 2. Of those that a mesh axis runs over, the one named last changes fastest.
Arguments:
- row_ids: int32 [32], P('row'), may hold values from -1 to 31, as said below
- a_tiles: bfloat16 [2048, 1024], P('row', 'col'), may hold values from -6 to 6
- a_mask: int32 [32, 16], P('row', 'col'), may hold values 0 or 1
- b_tiles: bfloat16 [1024, 6144], P('row', 'col'), may hold values from -0.375 to 0.375
- b_mask: int32 [16, 96], P('row', 'col'), may hold values 0 or 1
- c_keep: int32 [32, 96], P(None, 'col'), may hold values 0 or 1
Outputs:
- product_out: bfloat16 [2048, 6144], P('row', 'col')
Inputs may be any that keep to these rules, and one draw needn't show every extreme that they name: `row_ids`: within a group of 8 slots the live ids come first and -1 fills the rest; live ids are distinct over all slots; every group has at least half of its slots live and some group has all 8 live.
All inputs are finite; a program needn't handle non-finite values. No bound on the sum of `a_mask` or of `b_mask` or of `c_keep` on one device may be relied on, other than what follows from the above.
Results may differ from a plain program's by a relative error of at most 0.001.
Values may be sent and summed in bfloat16 or wider, within the bound.
No kernel may reach another device: no remote copies, remote signals or barrier semaphores. Data moves between devices by JAX's collectives and lax.ppermute only.
A program may use at most 64 MiB of HBM per device.

v0:
```python
import jax
import jax.numpy as jnp
from jax import lax
from jax.sharding import PartitionSpec as P

TILE = 64


def passed_along(block, axis, distance):
    devices = range(lax.axis_size(axis))
    route = [((i - distance) % len(devices), i) for i in devices]
    return lax.ppermute(block, axis, route)


def per_device(row_ids, a_tiles, a_mask, b_tiles, b_mask, c_keep):
    col_count = lax.axis_size("col")
    row_count = lax.axis_size("row")
    ratio_cols = col_count // row_count
    tile_edge = TILE
    slot_count = a_mask.shape[0]
    panel_blocks = a_mask.shape[1]
    column_blocks = b_mask.shape[1]
    panel_rows = panel_blocks * tile_edge
    a_eff = (
        a_tiles.reshape(slot_count, tile_edge, panel_blocks, tile_edge)
        * a_mask.astype(jnp.bfloat16)[:, None, :, None]
    )
    a_eff = a_eff.reshape(a_tiles.shape)
    b_eff = (
        b_tiles.reshape(b_mask.shape[0], tile_edge, column_blocks, tile_edge)
        * b_mask.astype(jnp.bfloat16)[:, None, :, None]
    )
    b_eff = b_eff.reshape(b_tiles.shape)
    running = jnp.zeros((a_tiles.shape[0], b_tiles.shape[1]), jnp.float32)

    def outer_step(group_step, carry):
        total, a_current, b_current = carry
        for inner_step in range(ratio_cols):
            local_panel = ratio_cols - 1 - inner_step
            b_rows = b_current[local_panel * panel_rows : (local_panel + 1) * panel_rows]
            total = total + jnp.dot(a_current, b_rows, preferred_element_type=jnp.float32)
            a_current = passed_along(a_current, "col", 1)
        b_current = passed_along(b_current, "row", 1)
        return (total, a_current, b_current)

    running, a_last, b_last = lax.fori_loop(0, row_count, outer_step, (running, a_eff, b_eff))
    onehot = (row_ids[:, None] == jnp.arange(c_keep.shape[0], dtype=jnp.int32)[None, :]).astype(
        jnp.float32
    )
    keep = jnp.dot(onehot, c_keep.astype(jnp.float32))
    masked = (
        running.reshape(slot_count, tile_edge, column_blocks, tile_edge) * keep[:, None, :, None]
    )
    return masked.reshape(running.shape).astype(jnp.bfloat16)


def solution(mesh):
    placed = (
        P("row"),
        P("row", "col"),
        P("row", "col"),
        P("row", "col"),
        P("row", "col"),
        P(None, "col"),
    )
    return jax.shard_map(
        per_device, mesh=mesh, in_specs=placed, out_specs=P("row", "col"), check_vma=False
    )
```

profile of v0, /device:TPU:0, one launch (start us, length us, event | category | flops | bytes accessed | tf_op | source)
XLA Modules:
  0.0 70.0 jit_solution(1124943943995114641)
XLA Ops:
  0.0 0.7 convert_element_type.13
  0.7 0.7 convert_element_type.14
  1.6 0.9 %fusion.4 = f32[8,12]{0,1:T(8,128)S(1)} fusion(s32[32,12]{0,1:T(8,128)} %param.13, s32[8]{0:T(128)} %param.8), kind=kOutput, calls=%fused_computation.6 | convolution fusion | flops 6784 | bytes 1952 | tf_op jit(solution)/shard_map/dot_general | solution.py:50
  2.5 0.2 mul.33
  2.7 0.1 mul.34
  2.8 1.6 %mul.35 = bf16[512,128]{1,0:T(8,128)(2,1)} multiply(bf16[512,128]{1,0:T(8,128)(2,1)} %param.9, bf16[512,128]{1,0:T(8,128)(2,1)S(1)} %mul.34) | non-fusion elementwise | flops 65536 | bytes 393216 | tf_op jit(solution)/shard_map/mul | solution.py:25
  4.4 1.2 %copy.10 = bf16[256,768]{0,1:T(8,128)(2,1)S(1)} copy(bf16[256,768]{1,0:T(8,128)(2,1)} %param.11) | data formatting | bytes 786432 | tf_op args[3]
  5.6 0.3 mul.36
  5.9 0.5 mul.37
  6.3 0.1 mul.38
  6.4 0.9 %copy.11 = bf16[256,768]{1,0:T(8,128)(2,1)} copy(bf16[256,768]{0,1:T(8,128)(2,1)S(1)} %mul.38) | data formatting | bytes 786432
  7.4 55.7 %while.15 = (s32[]{:T(128)}, f32[512,768]{1,0:T(8,128)S(1)}, bf16[512,128]{1,0:T(8,128)(2,1)}, bf16[256,768]{1,0:T(8,128)(2,1)}, s32[]{:T(128)}, /*index=5*/s32[]{:T(128)}) while((s32[]{:T(128)}, f32[512,768]{1,0:T(8,128)S(1)}, bf16[512,128]{1,0:T(8,128)(2,1)}, bf16[256,768]{1,0:T(8,128)(2,1)}, s32[]{:T(128)}, ...), condition=%wide.region_1.0_spmd.clone, body=%wide.region_0.0_spmd.clone.sunk | while | flops 202506240 | bytes 10354887 | solution.py:46
  7.4 0.5 collective-permute-start
  7.8 1.0 %copy.23 = bf16[256,768]{1,0:T(8,128)(2,1)S(1)} copy(bf16[256,768]{1,0:T(8,128)(2,1)} %get-tuple-element.89) | data formatting | bytes 786432 | tf_op jit(solution)/shard_map/while
  8.8 2.5 %collective-permute-start.2 = (bf16[256,768]{1,0:T(8,128)(2,1)S(1)}, bf16[256,768]{1,0:T(8,128)(2,1)}, u32[]{:S(2)}, u32[]{:S(2)}) collective-permute-start(bf16[256,768]{1,0:T(8,128)(2,1)S(1)} %copy.23), channel_id=1, source_target_pairs={{24,0},{0,8},{8,16},{16,24},{25,1},{1,9},{9,17},{17,25},{26,2},{2,... | collective-permute-start | bytes 1179656 | tf_op jit(solution)/shard_map/while/body/eval_jaxpr/ppermute | solution.py:12
  11.3 1.2 %fusion.19 = f32[512,768]{1,0:T(8,128)S(1)} fusion(bf16[512,128]{1,0:T(8,128)(2,1)} %get-tuple-element.88, bf16[256,768]{1,0:T(8,128)(2,1)S(1)} %copy.23), kind=kOutput, calls=%fused_computation.3.clone.1 | convolution fusion | flops 100663296 | bytes 1900544 | tf_op jit(solution)/shard_map/while/body/eval_jaxpr/dot_general | solution.py:41
  12.6 2.3 %collective-permute-done = bf16[512,128]{1,0:T(8,128)(2,1)} collective-permute-done((bf16[512,128]{1,0:T(8,128)(2,1)}, bf16[512,128]{1,0:T(8,128)(2,1)}, u32[]{:S(2)}, u32[]{:S(2)}) %collective-permute-start) | collective-permute-done | bytes 131104 | tf_op jit(solution)/shard_map/while/body/eval_jaxpr/ppermute | solution.py:12
  14.8 1.3 %fusion.20 = f32[512,768]{1,0:T(8,128)S(1)} fusion(f32[512,768]{1,0:T(8,128)S(1)} %fusion.19, f32[512,768]{1,0:T(8,128)S(1)} %get-tuple-element.87, bf16[512,128]{1,0:T(8,128)(2,1)} %collective-permute-done, pred[]{:T(512)S(6)} %compare.3, bf16[256,768]{1,0:T(8,128)(2,1)S(1)} %copy.23), kind=kOutput, calls=%fused_computation.1.clone.1 | convolution fusion | flops 101842944 | bytes 5046273 | tf_op jit(solution)/shard_map/while/body/eval_jaxpr/dot_general | solution.py:41
  16.1 5.2 %collective-permute-done.1 = bf16[512,128]{1,0:T(8,128)(2,1)} collective-permute-done((bf16[512,128]{1,0:T(8,128)(2,1)}, bf16[512,128]{1,0:T(8,128)(2,1)}, u32[]{:S(2)}, u32[]{:S(2)}) %collective-permute-start.1) | collective-permute-done | bytes 131104 | tf_op jit(solution)/shard_map/while/body/eval_jaxpr/ppermute | solution.py:12
  21.3 0.8 %collective-permute-start = (bf16[512,128]{1,0:T(8,128)(2,1)}, bf16[512,128]{1,0:T(8,128)(2,1)}, u32[]{:S(2)}, u32[]{:S(2)}) collective-permute-start(bf16[512,128]{1,0:T(8,128)(2,1)} %get-tuple-element.88), channel_id=1, source_target_pairs={{7,0},{0,1},{1,2},{2,3},{3,4},{4,5},{5,6},{6,7},{15,8},{8,9},{9,10... | collective-permute-start | bytes 393224 | tf_op jit(solution)/shard_map/while/body/eval_jaxpr/ppermute | solution.py:12
  22.2 1.0 %copy.23 = bf16[256,768]{1,0:T(8,128)(2,1)S(1)} copy(bf16[256,768]{1,0:T(8,128)(2,1)} %get-tuple-element.89) | data formatting | bytes 786432 | tf_op jit(solution)/shard_map/while
  23.2 1.3 %collective-permute-start.2 = (bf16[256,768]{1,0:T(8,128)(2,1)S(1)}, bf16[256,768]{1,0:T(8,128)(2,1)}, u32[]{:S(2)}, u32[]{:S(2)}) collective-permute-start(bf16[256,768]{1,0:T(8,128)(2,1)S(1)} %copy.23), channel_id=1, source_target_pairs={{24,0},{0,8},{8,16},{16,24},{25,1},{1,9},{9,17},{17,25},{26,2},{2,... | collective-permute-start | bytes 1179656 | tf_op jit(solution)/shard_map/while/body/eval_jaxpr/ppermute | solution.py:12
  24.4 1.3 %fusion.19 = f32[512,768]{1,0:T(8,128)S(1)} fusion(bf16[512,128]{1,0:T(8,128)(2,1)} %get-tuple-element.88, bf16[256,768]{1,0:T(8,128)(2,1)S(1)} %copy.23), kind=kOutput, calls=%fused_computation.3.clone.1 | convolution fusion | flops 100663296 | bytes 1900544 | tf_op jit(solution)/shard_map/while/body/eval_jaxpr/dot_general | solution.py:41
  25.7 2.1 %collective-permute-done = bf16[512,128]{1,0:T(8,128)(2,1)} collective-permute-done((bf16[512,128]{1,0:T(8,128)(2,1)}, bf16[512,128]{1,0:T(8,128)(2,1)}, u32[]{:S(2)}, u32[]{:S(2)}) %collective-permute-start) | collective-permute-done | bytes 131104 | tf_op jit(solution)/shard_map/while/body/eval_jaxpr/ppermute | solution.py:12
  27.9 1.3 %fusion.20 = f32[512,768]{1,0:T(8,128)S(1)} fusion(f32[512,768]{1,0:T(8,128)S(1)} %fusion.19, f32[512,768]{1,0:T(8,128)S(1)} %get-tuple-element.87, bf16[512,128]{1,0:T(8,128)(2,1)} %collective-permute-done, pred[]{:T(512)S(6)} %compare.3, bf16[256,768]{1,0:T(8,128)(2,1)S(1)} %copy.23), kind=kOutput, calls=%fused_computation.1.clone.1 | convolution fusion | flops 101842944 | bytes 5046273 | tf_op jit(solution)/shard_map/while/body/eval_jaxpr/dot_general | solution.py:41
  29.1 5.2 %collective-permute-done.1 = bf16[512,128]{1,0:T(8,128)(2,1)} collective-permute-done((bf16[512,128]{1,0:T(8,128)(2,1)}, bf16[512,128]{1,0:T(8,128)(2,1)}, u32[]{:S(2)}, u32[]{:S(2)}) %collective-permute-start.1) | collective-permute-done | bytes 131104 | tf_op jit(solution)/shard_map/while/body/eval_jaxpr/ppermute | solution.py:12
  34.4 1.1 %collective-permute-done.2 = bf16[256,768]{1,0:T(8,128)(2,1)} collective-permute-done((bf16[256,768]{1,0:T(8,128)(2,1)S(1)}, bf16[256,768]{1,0:T(8,128)(2,1)}, u32[]{:S(2)}, u32[]{:S(2)}) %collective-permute-start.2) | collective-permute-done | bytes 393248 | tf_op jit(solution)/shard_map/while/body/eval_jaxpr/ppermute | solution.py:12
  35.5 0.5 collective-permute-start
  36.0 1.0 %copy.23 = bf16[256,768]{1,0:T(8,128)(2,1)S(1)} copy(bf16[256,768]{1,0:T(8,128)(2,1)} %get-tuple-element.89) | data formatting | bytes 786432 | tf_op jit(solution)/shard_map/while
  37.0 0.7 collective-permute-start.2
  37.6 1.2 %fusion.19 = f32[512,768]{1,0:T(8,128)S(1)} fusion(bf16[512,128]{1,0:T(8,128)(2,1)} %get-tuple-element.88, bf16[256,768]{1,0:T(8,128)(2,1)S(1)} %copy.23), kind=kOutput, calls=%fused_computation.3.clone.1 | convolution fusion | flops 100663296 | bytes 1900544 | tf_op jit(solution)/shard_map/while/body/eval_jaxpr/dot_general | solution.py:41
  38.9 3.1 %collective-permute-done = bf16[512,128]{1,0:T(8,128)(2,1)} collective-permute-done((bf16[512,128]{1,0:T(8,128)(2,1)}, bf16[512,128]{1,0:T(8,128)(2,1)}, u32[]{:S(2)}, u32[]{:S(2)}) %collective-permute-start) | collective-permute-done | bytes 131104 | tf_op jit(solution)/shard_map/while/body/eval_jaxpr/ppermute | solution.py:12
  42.0 1.3 %fusion.20 = f32[512,768]{1,0:T(8,128)S(1)} fusion(f32[512,768]{1,0:T(8,128)S(1)} %fusion.19, f32[512,768]{1,0:T(8,128)S(1)} %get-tuple-element.87, bf16[512,128]{1,0:T(8,128)(2,1)} %collective-permute-done, pred[]{:T(512)S(6)} %compare.3, bf16[256,768]{1,0:T(8,128)(2,1)S(1)} %copy.23), kind=kOutput, calls=%fused_computation.1.clone.1 | convolution fusion | flops 101842944 | bytes 5046273 | tf_op jit(solution)/shard_map/while/body/eval_jaxpr/dot_general | solution.py:41
  43.3 5.2 %collective-permute-done.1 = bf16[512,128]{1,0:T(8,128)(2,1)} collective-permute-done((bf16[512,128]{1,0:T(8,128)(2,1)}, bf16[512,128]{1,0:T(8,128)(2,1)}, u32[]{:S(2)}, u32[]{:S(2)}) %collective-permute-start.1) | collective-permute-done | bytes 131104 | tf_op jit(solution)/shard_map/while/body/eval_jaxpr/ppermute | solution.py:12
  48.5 0.3 collective-permute-done.2
  48.8 1.0 %collective-permute-start = (bf16[512,128]{1,0:T(8,128)(2,1)}, bf16[512,128]{1,0:T(8,128)(2,1)}, u32[]{:S(2)}, u32[]{:S(2)}) collective-permute-start(bf16[512,128]{1,0:T(8,128)(2,1)} %get-tuple-element.88), channel_id=1, source_target_pairs={{7,0},{0,1},{1,2},{2,3},{3,4},{4,5},{5,6},{6,7},{15,8},{8,9},{9,10... | collective-permute-start | bytes 393224 | tf_op jit(solution)/shard_map/while/body/eval_jaxpr/ppermute | solution.py:12
  49.8 1.0 %copy.23 = bf16[256,768]{1,0:T(8,128)(2,1)S(1)} copy(bf16[256,768]{1,0:T(8,128)(2,1)} %get-tuple-element.89) | data formatting | bytes 786432 | tf_op jit(solution)/shard_map/while
  50.8 0.3 collective-permute-start.2
  51.1 1.2 %fusion.19 = f32[512,768]{1,0:T(8,128)S(1)} fusion(bf16[512,128]{1,0:T(8,128)(2,1)} %get-tuple-element.88, bf16[256,768]{1,0:T(8,128)(2,1)S(1)} %copy.23), kind=kOutput, calls=%fused_computation.3.clone.1 | convolution fusion | flops 100663296 | bytes 1900544 | tf_op jit(solution)/shard_map/while/body/eval_jaxpr/dot_general | solution.py:41
  52.4 2.9 %collective-permute-done = bf16[512,128]{1,0:T(8,128)(2,1)} collective-permute-done((bf16[512,128]{1,0:T(8,128)(2,1)}, bf16[512,128]{1,0:T(8,128)(2,1)}, u32[]{:S(2)}, u32[]{:S(2)}) %collective-permute-start) | collective-permute-done | bytes 131104 | tf_op jit(solution)/shard_map/while/body/eval_jaxpr/ppermute | solution.py:12
  55.3 1.3 %fusion.20 = f32[512,768]{1,0:T(8,128)S(1)} fusion(f32[512,768]{1,0:T(8,128)S(1)} %fusion.19, f32[512,768]{1,0:T(8,128)S(1)} %get-tuple-element.87, bf16[512,128]{1,0:T(8,128)(2,1)} %collective-permute-done, pred[]{:T(512)S(6)} %compare.3, bf16[256,768]{1,0:T(8,128)(2,1)S(1)} %copy.23), kind=kOutput, calls=%fused_computation.1.clone.1 | convolution fusion | flops 101842944 | bytes 5046273 | tf_op jit(solution)/shard_map/while/body/eval_jaxpr/dot_general | solution.py:41
  56.6 5.2 %collective-permute-done.1 = bf16[512,128]{1,0:T(8,128)(2,1)} collective-permute-done((bf16[512,128]{1,0:T(8,128)(2,1)}, bf16[512,128]{1,0:T(8,128)(2,1)}, u32[]{:S(2)}, u32[]{:S(2)}) %collective-permute-start.1) | collective-permute-done | bytes 131104 | tf_op jit(solution)/shard_map/while/body/eval_jaxpr/ppermute | solution.py:12
  61.8 1.3 %collective-permute-done.2 = bf16[256,768]{1,0:T(8,128)(2,1)} collective-permute-done((bf16[256,768]{1,0:T(8,128)(2,1)S(1)}, bf16[256,768]{1,0:T(8,128)(2,1)}, u32[]{:S(2)}, u32[]{:S(2)}) %collective-permute-start.2) | collective-permute-done | bytes 393248 | tf_op jit(solution)/shard_map/while/body/eval_jaxpr/ppermute | solution.py:12
  63.1 1.6 %copy.13 = f32[512,768]{0,1:T(8,128)} copy(f32[512,768]{1,0:T(8,128)S(1)} %get-tuple-element.27) | data formatting | bytes 3145728 | tf_op jit(solution)/shard_map/while | solution.py:46
  64.8 0.3 mul.39
  65.0 1.7 %mul.40 = f32[512,768]{0,1:T(8,128)} reshape(f32[8,64,12,64]{1,0,3,2:T(8,128)S(1)} %mul.39) | data formatting | bytes 3145728 | tf_op jit(solution)/shard_map/mul | solution.py:52
  66.7 2.1 %multiply_convert_fusion = bf16[512,768]{0,1:T(8,128)(2,1)S(1)} fusion(f32[512,768]{0,1:T(8,128)} %copy.13, f32[512,768]{0,1:T(8,128)} %mul.40), kind=kLoop, calls=%fused_computation.5 | loop fusion | flops 786432 | bytes 3932160 | tf_op jit(solution)/shard_map/convert_element_type | solution.py:54
  68.9 1.2 %copy.14 = bf16[512,768]{1,0:T(8,128)(2,1)} copy(bf16[512,768]{0,1:T(8,128)(2,1)S(1)} %multiply_convert_fusion) | data formatting | bytes 1572864 | tf_op jit(solution)/shard_map/convert_element_type | solution.py:54
  (8 shorter events, 0.2 us)
Async XLA Ops:
  7.4 7.5 %collective-permute-start = (bf16[512,128]{1,0:T(8,128)(2,1)}, bf16[512,128]{1,0:T(8,128)(2,1)}, u32[]{:S(2)}, u32[]{:S(2)}) collective-permute-start(bf16[512,128]{1,0:T(8,128)(2,1)} %get-tuple-element.88), channel_id=1, source_target_pairs={{7,0},{0,1},{1,2},{2,3},{3,4},{4,5},{5,6},{6,7},{15,8},{8,9},{9,10... | collective-permute-start | bytes 393224 | tf_op jit(solution)/shard_map/while/body/eval_jaxpr/ppermute | solution.py:12
  8.8 12.5 %collective-permute-start.2 = (bf16[256,768]{1,0:T(8,128)(2,1)S(1)}, bf16[256,768]{1,0:T(8,128)(2,1)}, u32[]{:S(2)}, u32[]{:S(2)}) collective-permute-start(bf16[256,768]{1,0:T(8,128)(2,1)S(1)} %copy.23), channel_id=1, source_target_pairs={{24,0},{0,8},{8,16},{16,24},{25,1},{1,9},{9,17},{17,25},{26,2},{2,... | collective-permute-start | bytes 1179656 | tf_op jit(solution)/shard_map/while/body/eval_jaxpr/ppermute | solution.py:12
  14.8 6.5 %collective-permute-start.1 = (bf16[512,128]{1,0:T(8,128)(2,1)}, bf16[512,128]{1,0:T(8,128)(2,1)}, u32[]{:S(2)}, u32[]{:S(2)}) collective-permute-start(bf16[512,128]{1,0:T(8,128)(2,1)} %collective-permute-done), channel_id=1, source_target_pairs={{7,0},{0,1},{1,2},{2,3},{3,4},{4,5},{5,6},{6,7},{15,8},{8,9},{9,10... | collective-permute-start | bytes 393224 | tf_op jit(solution)/shard_map/while/body/eval_jaxpr/ppermute | solution.py:12
  21.3 6.5 %collective-permute-start = (bf16[512,128]{1,0:T(8,128)(2,1)}, bf16[512,128]{1,0:T(8,128)(2,1)}, u32[]{:S(2)}, u32[]{:S(2)}) collective-permute-start(bf16[512,128]{1,0:T(8,128)(2,1)} %get-tuple-element.88), channel_id=1, source_target_pairs={{7,0},{0,1},{1,2},{2,3},{3,4},{4,5},{5,6},{6,7},{15,8},{8,9},{9,10... | collective-permute-start | bytes 393224 | tf_op jit(solution)/shard_map/while/body/eval_jaxpr/ppermute | solution.py:12
  23.2 12.3 %collective-permute-start.2 = (bf16[256,768]{1,0:T(8,128)(2,1)S(1)}, bf16[256,768]{1,0:T(8,128)(2,1)}, u32[]{:S(2)}, u32[]{:S(2)}) collective-permute-start(bf16[256,768]{1,0:T(8,128)(2,1)S(1)} %copy.23), channel_id=1, source_target_pairs={{24,0},{0,8},{8,16},{16,24},{25,1},{1,9},{9,17},{17,25},{26,2},{2,... | collective-permute-start | bytes 1179656 | tf_op jit(solution)/shard_map/while/body/eval_jaxpr/ppermute | solution.py:12
  27.9 6.5 %collective-permute-start.1 = (bf16[512,128]{1,0:T(8,128)(2,1)}, bf16[512,128]{1,0:T(8,128)(2,1)}, u32[]{:S(2)}, u32[]{:S(2)}) collective-permute-start(bf16[512,128]{1,0:T(8,128)(2,1)} %collective-permute-done), channel_id=1, source_target_pairs={{7,0},{0,1},{1,2},{2,3},{3,4},{4,5},{5,6},{6,7},{15,8},{8,9},{9,10... | collective-permute-start | bytes 393224 | tf_op jit(solution)/shard_map/while/body/eval_jaxpr/ppermute | solution.py:12
  35.5 6.5 %collective-permute-start = (bf16[512,128]{1,0:T(8,128)(2,1)}, bf16[512,128]{1,0:T(8,128)(2,1)}, u32[]{:S(2)}, u32[]{:S(2)}) collective-permute-start(bf16[512,128]{1,0:T(8,128)(2,1)} %get-tuple-element.88), channel_id=1, source_target_pairs={{7,0},{0,1},{1,2},{2,3},{3,4},{4,5},{5,6},{6,7},{15,8},{8,9},{9,10... | collective-permute-start | bytes 393224 | tf_op jit(solution)/shard_map/while/body/eval_jaxpr/ppermute | solution.py:12
  37.0 11.8 %collective-permute-start.2 = (bf16[256,768]{1,0:T(8,128)(2,1)S(1)}, bf16[256,768]{1,0:T(8,128)(2,1)}, u32[]{:S(2)}, u32[]{:S(2)}) collective-permute-start(bf16[256,768]{1,0:T(8,128)(2,1)S(1)} %copy.23), channel_id=1, source_target_pairs={{24,0},{0,8},{8,16},{16,24},{25,1},{1,9},{9,17},{17,25},{26,2},{2,... | collective-permute-start | bytes 1179656 | tf_op jit(solution)/shard_map/while/body/eval_jaxpr/ppermute | solution.py:12
  42.0 6.5 %collective-permute-start.1 = (bf16[512,128]{1,0:T(8,128)(2,1)}, bf16[512,128]{1,0:T(8,128)(2,1)}, u32[]{:S(2)}, u32[]{:S(2)}) collective-permute-start(bf16[512,128]{1,0:T(8,128)(2,1)} %collective-permute-done), channel_id=1, source_target_pairs={{7,0},{0,1},{1,2},{2,3},{3,4},{4,5},{5,6},{6,7},{15,8},{8,9},{9,10... | collective-permute-start | bytes 393224 | tf_op jit(solution)/shard_map/while/body/eval_jaxpr/ppermute | solution.py:12
  48.8 6.5 %collective-permute-start = (bf16[512,128]{1,0:T(8,128)(2,1)}, bf16[512,128]{1,0:T(8,128)(2,1)}, u32[]{:S(2)}, u32[]{:S(2)}) collective-permute-start(bf16[512,128]{1,0:T(8,128)(2,1)} %get-tuple-element.88), channel_id=1, source_target_pairs={{7,0},{0,1},{1,2},{2,3},{3,4},{4,5},{5,6},{6,7},{15,8},{8,9},{9,10... | collective-permute-start | bytes 393224 | tf_op jit(solution)/shard_map/while/body/eval_jaxpr/ppermute | solution.py:12
  50.8 12.3 %collective-permute-start.2 = (bf16[256,768]{1,0:T(8,128)(2,1)S(1)}, bf16[256,768]{1,0:T(8,128)(2,1)}, u32[]{:S(2)}, u32[]{:S(2)}) collective-permute-start(bf16[256,768]{1,0:T(8,128)(2,1)S(1)} %copy.23), channel_id=1, source_target_pairs={{24,0},{0,8},{8,16},{16,24},{25,1},{1,9},{9,17},{17,25},{26,2},{2,... | collective-permute-start | bytes 1179656 | tf_op jit(solution)/shard_map/while/body/eval_jaxpr/ppermute | solution.py:12
  55.3 6.5 %collective-permute-start.1 = (bf16[512,128]{1,0:T(8,128)(2,1)}, bf16[512,128]{1,0:T(8,128)(2,1)}, u32[]{:S(2)}, u32[]{:S(2)}) collective-permute-start(bf16[512,128]{1,0:T(8,128)(2,1)} %collective-permute-done), channel_id=1, source_target_pairs={{7,0},{0,1},{1,2},{2,3},{3,4},{4,5},{5,6},{6,7},{15,8},{8,9},{9,10... | collective-permute-start | bytes 393224 | tf_op jit(solution)/shard_map/while/body/eval_jaxpr/ppermute | solution.py:12
where the time goes:
time: 70.6 us; the launch traced here: 70 us
  waiting for transfers between devices  34.1 us (48%)
  local copies, waits for them, and re-layouts  12.1 us (17%)
  matrix products  11 us (16%)
  starting transfers between devices  7.51 us (11%)
  other arithmetic  5.18 us (7%)
    ppermute x12, waiting for transfers between devices, passed_along(): return lax.ppermute(block, axis, route)  34.1 us
    dot_general x8, matrix products, outer_step(): jnp.dot(a_current, b_rows, preferred_element_type=jnp.float32)  10.1 us
    ppermute x12, starting transfers between devices, passed_along(): return lax.ppermute(block, axis, route)  7.51 us
    while x4, local copies, waits for them, and re-layouts  3.98 us
    convert_element_type x1, other arithmetic, per_device(): return masked.reshape(running.shape).astype(jnp.bfloat16)  2.13 us
    unnamed x2, local copies, waits for them, and re-layouts  2.09 us
    mul x2, local copies, waits for them, and re-layouts, per_device(): running.reshape(slot_count, tile_edge, column_blocks, tile_edge)  1.96 us
    while x1, local copies, waits for them, and re-layouts, per_device(): lax.fori_loop(0, row_count, outer_step, (running, a_eff, b_eff))  1.64 us
  transfers between devices with their start and end apart: 12, of which 11 were waited for; matrix products, arithmetic and copies ran while one was open for 20% of the time, Pallas kernels for 0%

commit v1 on v0

v1 whole, which is shorter than its diff:
```python
import functools

import jax
import jax.numpy as jnp
from jax import lax
from jax.experimental import pallas as pl
from jax.experimental.pallas import tpu as pltpu
from jax.sharding import PartitionSpec as P

TILE = 64
ANY = pl.BlockSpec(memory_space=pl.ANY)
VMEM = pl.BlockSpec(memory_space=pltpu.VMEM)
SMEM = pl.BlockSpec(memory_space=pltpu.SMEM)


def spread_matrix(blocks):
    shape = (blocks, blocks * TILE)
    owner = lax.broadcasted_iota(jnp.int32, shape, 1) // TILE
    return (owner == lax.broadcasted_iota(jnp.int32, shape, 0)).astype(jnp.float32)


def spread(mask):
    return jnp.dot(
        mask.astype(jnp.float32), spread_matrix(mask.shape[1]), preferred_element_type=jnp.float32
    )


def mask_kernel(parts, mask_ref, tiles_ref, *out_refs):
    wide = spread(mask_ref[...]).astype(jnp.bfloat16)
    rows = tiles_ref.shape[0] // parts
    for part, out_ref in enumerate(out_refs):
        for i in range(rows // TILE):
            block = (part * rows) // TILE + i
            source = pl.ds(block * TILE, TILE)
            out_ref[pl.ds(i * TILE, TILE), :] = tiles_ref[source, :] * wide[block : block + 1, :]


def masked(mask, tiles, parts):
    part = jax.ShapeDtypeStruct((tiles.shape[0] // parts, tiles.shape[1]), tiles.dtype)
    return pl.pallas_call(
        functools.partial(mask_kernel, parts),
        out_shape=(part,) * parts,
        in_specs=[VMEM, VMEM],
        out_specs=(VMEM,) * parts,
        cost_estimate=pl.CostEstimate(
            flops=tiles.size, bytes_accessed=4 * tiles.size, transcendentals=0
        ),
    )(mask, tiles)


def product_kernel(
    a_sources, b_pieces, mesh_sizes, row_ids_ref, c_keep_ref, *refs
):
    row_count, col_count = mesh_sizes
    ratio = col_count // row_count
    a_refs = refs[: len(a_sources)]
    b_refs = refs[len(a_sources) : len(a_sources) + len(b_pieces)]
    out_ref, a_all, b_all, out_tile, keep_wide, in_sem, out_sem = refs[
        len(a_sources) + len(b_pieces) :
    ]
    me_row, me_col = lax.axis_index("row"), lax.axis_index("col")
    width = a_all.shape[1] // col_count
    copies = []
    for distance, a_ref in zip(a_sources, a_refs, strict=True):
        stored = me_col ^ distance
        inner = lax.rem(stored + ratio * me_row + ratio - 1, col_count)
        columns = pl.ds(pl.multiple_of(inner * width, width), width)
        copies.append((a_ref, a_all.at[:, columns]))
    for (distance, first), b_ref in zip(b_pieces, b_refs, strict=True):
        piece = min(width, b_ref.shape[0])
        for start in range(0, b_ref.shape[0], piece):
            place = first + start
            stored = (me_row ^ distance) * ratio + place // width
            inner = lax.rem(stored + me_col, col_count)
            rows = pl.ds(pl.multiple_of(inner * width + place % width, piece), piece)
            copies.append((b_ref.at[pl.ds(start, piece), :], b_all.at[rows, :]))
    copies = [
        pltpu.make_async_copy(source, target, in_sem.at[i])
        for i, (source, target) in enumerate(copies)
    ]
    for copy in copies:
        copy.start()

    rows_live = row_ids_ref[...]
    which = lax.broadcasted_iota(jnp.int32, (rows_live.shape[0], c_keep_ref.shape[0]), 1)
    onehot = (rows_live == which).astype(jnp.float32)
    keep = jnp.dot(
        onehot, c_keep_ref[...].astype(jnp.float32), preferred_element_type=jnp.float32
    )
    keep_wide[...] = spread(keep)

    for copy in copies:
        copy.wait()
    rows = out_tile.shape[1]
    writes = []
    for step in range(a_all.shape[0] // rows):
        total = jnp.dot(
            a_all[pl.ds(step * rows, rows), :], b_all[...], preferred_element_type=jnp.float32
        )
        for i in range(rows // TILE):
            slot = step * rows // TILE + i
            out_tile[step, pl.ds(i * TILE, TILE), :] = (
                total[i * TILE : (i + 1) * TILE] * keep_wide[pl.ds(slot, 1), :]
            ).astype(jnp.bfloat16)
        writes.append(
            pltpu.make_async_copy(
                out_tile.at[step], out_ref.at[pl.ds(step * rows, rows), :], out_sem.at[step]
            )
        )
        writes[-1].start()
    for write in writes:
        write.wait()


def product(row_ids, c_keep, a_blocks, b_blocks, mesh_sizes):
    a_rows, width = a_blocks[0].shape
    columns = next(iter(b_blocks.values())).shape[1]
    inner = width * mesh_sizes[1]
    rows = 2 * TILE
    steps = a_rows // rows
    n_copies = len(a_blocks) + sum(-(-b.shape[0] // width) for b in b_blocks.values())
    return pl.pallas_call(
        functools.partial(product_kernel, tuple(a_blocks), tuple(b_blocks), mesh_sizes),
        out_shape=jax.ShapeDtypeStruct((a_rows, columns), jnp.bfloat16),
        in_specs=[VMEM, VMEM] + [ANY] * (len(a_blocks) + len(b_blocks)),
        out_specs=ANY,
        scratch_shapes=[
            pltpu.VMEM((a_rows, inner), jnp.bfloat16),
            pltpu.VMEM((inner, columns), jnp.bfloat16),
            pltpu.VMEM((steps, rows, columns), jnp.bfloat16),
            pltpu.VMEM((a_rows // TILE, columns), jnp.float32),
            pltpu.SemaphoreType.DMA((n_copies,)),
            pltpu.SemaphoreType.DMA((steps,)),
        ],
        compiler_params=pltpu.CompilerParams(vmem_limit_bytes=32 * 1024 * 1024),
        cost_estimate=pl.CostEstimate(
            flops=2 * a_rows * inner * columns,
            bytes_accessed=2 * (a_rows * inner + inner * columns + a_rows * columns),
            transcendentals=0,
        ),
    )(row_ids[:, None], c_keep, *a_blocks.values(), *b_blocks.values())


def swapped(block, axis, distance):
    return lax.ppermute(block, axis, [(i, i ^ distance) for i in range(lax.axis_size(axis))])


def gathered_b(b_eff):
    row_count = lax.axis_size("row")
    rows = b_eff.shape[0]
    half = rows // 2
    if row_count != 4:
        pieces = {(d, 0): swapped(b_eff, "row", d) for d in range(1, row_count)}
        return {(0, 0): b_eff, **pieces}
    near, far = swapped(b_eff, "row", 1), swapped(b_eff, "row", 2)
    return {
        (0, 0): b_eff,
        (1, 0): near,
        (2, 0): far,
        (3, 0): swapped(near[:half], "row", 2),
        (3, half): swapped(far[half:], "row", 1),
    }


def gathered_a(a_eff):
    blocks = {0: a_eff}
    for distance in range(2, lax.axis_size("col"), 2):
        blocks[distance] = swapped(a_eff, "col", distance)
    for distance in tuple(blocks):
        blocks[distance + 1] = swapped(blocks[distance], "col", 1)
    return blocks


def per_device(row_ids, a_tiles, a_mask, b_tiles, b_mask, c_keep):
    (b_eff,) = masked(b_mask, b_tiles, 1)
    (a_eff,) = masked(a_mask, a_tiles, 1)
    return product(
        row_ids,
        c_keep,
        gathered_a(a_eff),
        gathered_b(b_eff),
        (lax.axis_size("row"), lax.axis_size("col")),
    )


def solution(mesh):
    placed = (
        P("row"),
        P("row", "col"),
        P("row", "col"),
        P("row", "col"),
        P("row", "col"),
        P(None, "col"),
    )
    return jax.shard_map(
        per_device, mesh=mesh, in_specs=placed, out_specs=P("row", "col"), check_vma=False
    )
```

time: 70.6 us -> 31 us (0.44)
  waiting for transfers between devices: 34.1 us -> 7.79 us
  local copies, waits for them, and re-layouts: 12.1 us -> 0.88 us
  matrix products: 11 us -> 0 us
  Pallas kernels: 0 us -> 8.62 us
  starting transfers between devices: 7.51 us -> 13.5 us
  other arithmetic: 5.18 us -> 0 us
    ppermute x12 -> x11, waiting for transfers between devices: 34.1 us -> 7.79 us  [swapped(): lax.ppermute(block, axis, [(i, i ^ distance) for i in range(lax.axis_size...]
    dot_general x9 -> x0, matrix products: 11 us -> none  [the longest x8 10.1 us: outer_step(): jnp.dot(a_current, b_rows, preferred_element_type=jnp.float32)]
    pallas_call x0 -> x3, Pallas kernels: none -> 8.62 us  [the longest x1 4.99 us: product(): pl.pallas_call(functools.partial(product_kernel, tuple(a_blocks), tuple(b...]
    ppermute x12 -> x11, starting transfers between devices: 7.51 us -> 13.5 us  [swapped(): lax.ppermute(block, axis, [(i, i ^ distance) for i in range(lax.axis_size...]
    while x5 -> x0, local copies, waits for them, and re-layouts: 5.62 us -> none
    convert_element_type x3 -> x0, other arithmetic: 3.5 us -> none  [the longest x1 2.13 us: per_device(): return masked.reshape(running.shape).astype(jnp.bfloat16)]
    mul x6 -> x0, local copies, waits for them, and re-layouts: 3.05 us -> none  [the longest x2 1.96 us: per_device(): running.reshape(slot_count, tile_edge, column_blocks, tile_edge)]
    mul x2 -> x0, other arithmetic: 1.68 us -> none  [the longest x1 1.58 us: per_device(): a_tiles.reshape(slot_count, tile_edge, panel_blocks, tile_edge)]
  transfers between devices with their start and end apart: 12 -> 11, of which waited for: 11 -> 4; matrix products, arithmetic and copies ran while one was open for 20% -> 3% of each run, Pallas kernels for 0% -> 6%
where the time goes in v1:
time: 31 us; the launch traced here: 30.9 us
  starting transfers between devices  13.5 us (44%)
  Pallas kernels  8.62 us (28%)
  waiting for transfers between devices  7.79 us (25%)
  local copies, waits for them, and re-layouts  0.88 us (3%)
    ppermute x11, starting transfers between devices, swapped(): lax.ppermute(block, axis, [(i, i ^ distance) for i in range(lax.axis_size...  13.5 us
    ppermute x11, waiting for transfers between devices, swapped(): lax.ppermute(block, axis, [(i, i ^ distance) for i in range(lax.axis_size...  7.79 us
    pallas_call x1, Pallas kernels, product(): pl.pallas_call(functools.partial(product_kernel, tuple(a_blocks), tuple(b...  4.99 us
    pallas_call x2, Pallas kernels, masked(): pl.pallas_call(functools.partial(mask_kernel, parts), out_shape=(part,) *...  3.62 us
    unnamed x12, local copies, waits for them, and re-layouts  0.77 us
  transfers between devices with their start and end apart: 11, of which 4 were waited for; matrix products, arithmetic and copies ran while one was open for 3% of the time, Pallas kernels for 6%

profile of v1, /device:TPU:0, one launch (start us, length us, event | category | flops | bytes accessed | tf_op | source)
XLA Modules:
  0.0 30.9 jit_solution(13387188344158848810)
XLA Ops:
  0.0 0.0 copy-start.3
  0.0 1.9 %shard_map.65.refs_8_ = bf16[256,768]{1,0:T(8,128)(2,1)} custom-call(s32[4,12]{1,0:T(4,128)} %mask_ref.2, bf16[256,768]{1,0:T(8,128)(2,1)} %tiles_ref.3), custom_call_target="tpu_custom_call" | custom-call | flops 196608 | bytes 786432 | tf_op jit(solution)/shard_map/pallas_call | solution.py:40
  1.9 3.0 %collective-permute-start.8 = (bf16[256,768]{1,0:T(8,128)(2,1)}, bf16[256,768]{1,0:T(8,128)(2,1)S(1)}, u32[]{:S(2)}, u32[]{:S(2)}) collective-permute-start(bf16[256,768]{1,0:T(8,128)(2,1)} %shard_map.65.refs_8_), channel_id=1, source_target_pairs={{0,16},{8,24},{16,0},{24,8},{1,17},{9,25},{17,1},{25,9},{2,18},{10... | collective-permute-start | bytes 1179656 | tf_op jit(solution)/shard_map/ppermute | solution.py:145
  4.9 1.5 %collective-permute-start.7 = (bf16[256,768]{1,0:T(8,128)(2,1)}, bf16[256,768]{1,0:T(8,128)(2,1)S(1)}, u32[]{:S(2)}, u32[]{:S(2)}) collective-permute-start(bf16[256,768]{1,0:T(8,128)(2,1)} %shard_map.65.refs_8_), channel_id=1, source_target_pairs={{0,8},{8,0},{16,24},{24,16},{1,9},{9,1},{17,25},{25,17},{2,10},{10... | collective-permute-start | bytes 1179656 | tf_op jit(solution)/shard_map/ppermute | solution.py:145
  6.4 0.0 copy-done.3
  6.4 0.7 %copy.7.mask_ref = s32[8,2]{1,0:T(8,128)} copy(s32[8,2]{0,1:T(2,128)S(1)} %copy-done.3) | data formatting | bytes 128 | tf_op args[2]
  7.0 1.7 %shard_map.64.refs_0_ = bf16[512,128]{1,0:T(8,128)(2,1)} custom-call(s32[8,2]{1,0:T(8,128)} %copy.7.mask_ref, bf16[512,128]{1,0:T(8,128)(2,1)} %tiles_ref.2), custom_call_target="tpu_custom_call" | custom-call | flops 65536 | bytes 262144 | tf_op jit(solution)/shard_map/pallas_call | solution.py:40
  8.8 0.0 copy-start
  8.8 0.0 collective-permute-start.3
  8.8 3.6 %collective-permute-start.2 = (bf16[512,128]{1,0:T(8,128)(2,1)}, bf16[512,128]{1,0:T(8,128)(2,1)S(1)}, u32[]{:S(2)}, u32[]{:S(2)}) collective-permute-start(bf16[512,128]{1,0:T(8,128)(2,1)} %shard_map.64.refs_0_), channel_id=1, source_target_pairs={{0,6},{1,7},{2,4},{3,5},{4,2},{5,3},{6,0},{7,1},{8,14},{9,15},{10,... | collective-permute-start | bytes 393224 | tf_op jit(solution)/shard_map/ppermute | solution.py:145
  12.4 0.0 collective-permute-start.1
  12.4 1.8 %collective-permute-done.8.refs_10_ = bf16[256,768]{1,0:T(8,128)(2,1)S(1)} collective-permute-done((bf16[256,768]{1,0:T(8,128)(2,1)}, bf16[256,768]{1,0:T(8,128)(2,1)S(1)}, u32[]{:S(2)}, u32[]{:S(2)}) %collective-permute-start.8) | collective-permute-done | bytes 393248 | tf_op jit(solution)/shard_map/ppermute | solution.py:145
  14.2 1.8 %collective-permute-start = (bf16[512,128]{1,0:T(8,128)(2,1)}, bf16[512,128]{1,0:T(8,128)(2,1)S(1)}, u32[]{:S(2)}, u32[]{:S(2)}) collective-permute-start(bf16[512,128]{1,0:T(8,128)(2,1)} %shard_map.64.refs_0_), channel_id=1, source_target_pairs={{0,2},{1,3},{2,0},{3,1},{4,6},{5,7},{6,4},{7,5},{8,10},{9,11},{10,... | collective-permute-start | bytes 393224 | tf_op jit(solution)/shard_map/ppermute | solution.py:145
  16.0 0.0 copy-start.1
  16.0 0.0 collective-permute-done.7.refs_9_
  16.0 1.6 %collective-permute-start.10 = (bf16[128,768]{1,0:T(8,128)(2,1)S(1)}, bf16[128,768]{1,0:T(8,128)(2,1)S(1)}, u32[]{:S(2)}, u32[]{:S(2)}) collective-permute-start(bf16[128,768]{1,0:T(8,128)(2,1)S(1)} %slice.9), channel_id=1, source_target_pairs={{0,8},{8,0},{16,24},{24,16},{1,9},{9,1},{17,25},{25,17},{2,10},{10... | collective-permute-start | bytes 589832 | tf_op jit(solution)/shard_map/ppermute | solution.py:145
  17.6 0.0 copy-start.2
  17.6 0.0 copy-start.4
  17.6 0.0 collective-permute-done.3.refs_4_
  17.6 1.6 %collective-permute-start.9 = (bf16[128,768]{1,0:T(8,128)(2,1)S(1)}, bf16[128,768]{1,0:T(8,128)(2,1)S(1)}, u32[]{:S(2)}, u32[]{:S(2)}) collective-permute-start(bf16[128,768]{1,0:T(8,128)(2,1)S(1)} %slice.8), channel_id=1, source_target_pairs={{0,16},{8,24},{16,0},{24,8},{1,17},{9,25},{17,1},{25,9},{2,18},{10... | collective-permute-start | bytes 589832 | tf_op jit(solution)/shard_map/ppermute | solution.py:145
  19.2 0.0 collective-permute-done.2.refs_3_
  19.2 0.0 collective-permute-start.6
  19.2 5.1 %collective-permute-done.1.refs_2_ = bf16[512,128]{1,0:T(8,128)(2,1)S(1)} collective-permute-done((bf16[512,128]{1,0:T(8,128)(2,1)}, bf16[512,128]{1,0:T(8,128)(2,1)S(1)}, u32[]{:S(2)}, u32[]{:S(2)}) %collective-permute-start.1) | collective-permute-done | bytes 131104 | tf_op jit(solution)/shard_map/ppermute | solution.py:145
  24.3 0.0 collective-permute-start.5
  24.3 0.0 collective-permute-done.refs_1_
  24.3 0.5 %collective-permute-start.4 = (bf16[512,128]{1,0:T(8,128)(2,1)S(1)}, bf16[512,128]{1,0:T(8,128)(2,1)S(1)}, u32[]{:S(2)}, u32[]{:S(2)}) collective-permute-start(bf16[512,128]{1,0:T(8,128)(2,1)S(1)} %collective-permute-done.refs_1_), channel_id=1, source_target_pairs={{0,1},{1,0},{2,3},{3,2},{4,5},{5,4},{6,7},{7,6},{8,9},{9,8},{10,11... | collective-permute-start | bytes 393224 | tf_op jit(solution)/shard_map/ppermute | solution.py:145
  24.8 0.0 copy-done.4
  24.8 0.1 copy.8.row_ids_ref
  24.9 0.0 copy-done.2
  24.9 0.1 copy.9.c_keep_ref
  25.0 0.0 collective-permute-done.6.refs_7_
  25.0 0.7 %collective-permute-done.5.refs_6_ = bf16[512,128]{1,0:T(8,128)(2,1)S(1)} collective-permute-done((bf16[512,128]{1,0:T(8,128)(2,1)S(1)}, bf16[512,128]{1,0:T(8,128)(2,1)S(1)}, u32[]{:S(2)}, u32[]{:S(2)}) %collective-permute-start.5) | collective-permute-done | bytes 131104 | tf_op jit(solution)/shard_map/ppermute | solution.py:145
  25.7 0.2 collective-permute-done.4.refs_5_
  25.9 0.0 collective-permute-done.10.refs_12_
  25.9 0.0 collective-permute-done.9.refs_11_
  25.9 0.0 copy-done
  25.9 0.0 copy-done.1
  25.9 5.0 %shard_map.66 = bf16[512,768]{1,0:T(8,128)(2,1)} custom-call(s32[8,1]{1,0:T(8,128)S(1)} %copy.8.row_ids_ref, s32[32,12]{1,0:T(8,128)S(1)} %copy.9.c_keep_ref, bf16[512,128]{1,0:T(8,128)(2,1)S(1)} %copy-done.1, bf16[512,128]{1,0:T(8,128)(2,1)S(1)} %collective-permute-done.refs_1_, bf16[512,128]{1,0:T(8,128)(2,1)S(1)} %collective-permute-done.1.refs_2_, ...), custom_call_target="tpu_custom_call" | custom-call | flops 805306368 | bytes 3407872 | tf_op jit(solution)/shard_map/pallas_call | solution.py:122
  (2 shorter events, 0.0 us)
Async XLA Ops:
  0.0 6.4 %copy-start.3 = (s32[8,2]{0,1:T(2,128)S(1)}, s32[8,2]{0,1:T(2,128)}, u32[]{:S(2)}) copy-start(s32[8,2]{0,1:T(2,128)} %param.8) | copy-start | bytes 196
  1.9 12.3 %collective-permute-start.8 = (bf16[256,768]{1,0:T(8,128)(2,1)}, bf16[256,768]{1,0:T(8,128)(2,1)S(1)}, u32[]{:S(2)}, u32[]{:S(2)}) collective-permute-start(bf16[256,768]{1,0:T(8,128)(2,1)} %shard_map.65.refs_8_), channel_id=1, source_target_pairs={{0,16},{8,24},{16,0},{24,8},{1,17},{9,25},{17,1},{25,9},{2,18},{10... | collective-permute-start | bytes 1179656 | tf_op jit(solution)/shard_map/ppermute | solution.py:145
  4.9 11.2 %collective-permute-start.7 = (bf16[256,768]{1,0:T(8,128)(2,1)}, bf16[256,768]{1,0:T(8,128)(2,1)S(1)}, u32[]{:S(2)}, u32[]{:S(2)}) collective-permute-start(bf16[256,768]{1,0:T(8,128)(2,1)} %shard_map.65.refs_8_), channel_id=1, source_target_pairs={{0,8},{8,0},{16,24},{24,16},{1,9},{9,1},{17,25},{25,17},{2,10},{10... | collective-permute-start | bytes 1179656 | tf_op jit(solution)/shard_map/ppermute | solution.py:145
  8.8 17.1 %copy-start = (bf16[256,768]{1,0:T(8,128)(2,1)S(1)}, bf16[256,768]{1,0:T(8,128)(2,1)}, u32[]{:S(2)}) copy-start(bf16[256,768]{1,0:T(8,128)(2,1)} %shard_map.65.refs_8_) | copy-start | bytes 1179652
  8.8 8.9 %collective-permute-start.3 = (bf16[512,128]{1,0:T(8,128)(2,1)}, bf16[512,128]{1,0:T(8,128)(2,1)S(1)}, u32[]{:S(2)}, u32[]{:S(2)}) collective-permute-start(bf16[512,128]{1,0:T(8,128)(2,1)} %shard_map.64.refs_0_), channel_id=1, source_target_pairs={{0,1},{1,0},{2,3},{3,2},{4,5},{5,4},{6,7},{7,6},{8,9},{9,8},{10,11... | collective-permute-start | bytes 393224 | tf_op jit(solution)/shard_map/ppermute | solution.py:145
  8.8 10.5 %collective-permute-start.2 = (bf16[512,128]{1,0:T(8,128)(2,1)}, bf16[512,128]{1,0:T(8,128)(2,1)S(1)}, u32[]{:S(2)}, u32[]{:S(2)}) collective-permute-start(bf16[512,128]{1,0:T(8,128)(2,1)} %shard_map.64.refs_0_), channel_id=1, source_target_pairs={{0,6},{1,7},{2,4},{3,5},{4,2},{5,3},{6,0},{7,1},{8,14},{9,15},{10,... | collective-permute-start | bytes 393224 | tf_op jit(solution)/shard_map/ppermute | solution.py:145
  12.4 12.0 %collective-permute-start.1 = (bf16[512,128]{1,0:T(8,128)(2,1)}, bf16[512,128]{1,0:T(8,128)(2,1)S(1)}, u32[]{:S(2)}, u32[]{:S(2)}) collective-permute-start(bf16[512,128]{1,0:T(8,128)(2,1)} %shard_map.64.refs_0_), channel_id=1, source_target_pairs={{0,4},{1,5},{2,6},{3,7},{4,0},{5,1},{6,2},{7,3},{8,12},{9,13},{10,... | collective-permute-start | bytes 393224 | tf_op jit(solution)/shard_map/ppermute | solution.py:145
  14.2 10.1 %collective-permute-start = (bf16[512,128]{1,0:T(8,128)(2,1)}, bf16[512,128]{1,0:T(8,128)(2,1)S(1)}, u32[]{:S(2)}, u32[]{:S(2)}) collective-permute-start(bf16[512,128]{1,0:T(8,128)(2,1)} %shard_map.64.refs_0_), channel_id=1, source_target_pairs={{0,2},{1,3},{2,0},{3,1},{4,6},{5,7},{6,4},{7,5},{8,10},{9,11},{10,... | collective-permute-start | bytes 393224 | tf_op jit(solution)/shard_map/ppermute | solution.py:145
  16.0 9.8 %copy-start.1 = (bf16[512,128]{1,0:T(8,128)(2,1)S(1)}, bf16[512,128]{1,0:T(8,128)(2,1)}, u32[]{:S(2)}) copy-start(bf16[512,128]{1,0:T(8,128)(2,1)} %shard_map.64.refs_0_) | copy-start | bytes 393220
  16.0 9.8 %collective-permute-start.10 = (bf16[128,768]{1,0:T(8,128)(2,1)S(1)}, bf16[128,768]{1,0:T(8,128)(2,1)S(1)}, u32[]{:S(2)}, u32[]{:S(2)}) collective-permute-start(bf16[128,768]{1,0:T(8,128)(2,1)S(1)} %slice.9), channel_id=1, source_target_pairs={{0,8},{8,0},{16,24},{24,16},{1,9},{9,1},{17,25},{25,17},{2,10},{10... | collective-permute-start | bytes 589832 | tf_op jit(solution)/shard_map/ppermute | solution.py:145
  17.6 7.3 %copy-start.2 = (s32[32,12]{0,1:T(8,128)S(1)}, s32[32,12]{0,1:T(8,128)}, u32[]{:S(2)}) copy-start(s32[32,12]{0,1:T(8,128)} %param.11) | copy-start | bytes 4612
  17.6 7.2 %copy-start.4 = (s32[8]{0:T(128)S(1)}, s32[8]{0:T(128)}, u32[]{:S(2)}) copy-start(s32[8]{0:T(128)} %param.6) | copy-start | bytes 100
  17.6 8.2 %collective-permute-start.9 = (bf16[128,768]{1,0:T(8,128)(2,1)S(1)}, bf16[128,768]{1,0:T(8,128)(2,1)S(1)}, u32[]{:S(2)}, u32[]{:S(2)}) collective-permute-start(bf16[128,768]{1,0:T(8,128)(2,1)S(1)} %slice.8), channel_id=1, source_target_pairs={{0,16},{8,24},{16,0},{24,8},{1,17},{9,25},{17,1},{25,9},{2,18},{10... | collective-permute-start | bytes 589832 | tf_op jit(solution)/shard_map/ppermute | solution.py:145
  19.2 5.8 %collective-permute-start.6 = (bf16[512,128]{1,0:T(8,128)(2,1)S(1)}, bf16[512,128]{1,0:T(8,128)(2,1)S(1)}, u32[]{:S(2)}, u32[]{:S(2)}) collective-permute-start(bf16[512,128]{1,0:T(8,128)(2,1)S(1)} %collective-permute-done.2.refs_3_), channel_id=1, source_target_pairs={{0,1},{1,0},{2,3},{3,2},{4,5},{5,4},{6,7},{7,6},{8,9},{9,8},{10,11... | collective-permute-start | bytes 393224 | tf_op jit(solution)/shard_map/ppermute | solution.py:145
  24.3 1.3 %collective-permute-start.5 = (bf16[512,128]{1,0:T(8,128)(2,1)S(1)}, bf16[512,128]{1,0:T(8,128)(2,1)S(1)}, u32[]{:S(2)}, u32[]{:S(2)}) collective-permute-start(bf16[512,128]{1,0:T(8,128)(2,1)S(1)} %collective-permute-done.1.refs_2_), channel_id=1, source_target_pairs={{0,1},{1,0},{2,3},{3,2},{4,5},{5,4},{6,7},{7,6},{8,9},{9,8},{10,11... | collective-permute-start | bytes 393224 | tf_op jit(solution)/shard_map/ppermute | solution.py:145
  24.3 1.5 %collective-permute-start.4 = (bf16[512,128]{1,0:T(8,128)(2,1)S(1)}, bf16[512,128]{1,0:T(8,128)(2,1)S(1)}, u32[]{:S(2)}, u32[]{:S(2)}) collective-permute-start(bf16[512,128]{1,0:T(8,128)(2,1)S(1)} %collective-permute-done.refs_1_), channel_id=1, source_target_pairs={{0,1},{1,0},{2,3},{3,2},{4,5},{5,4},{6,7},{7,6},{8,9},{9,8},{10,11... | collective-permute-start | bytes 393224 | tf_op jit(solution)/shard_map/ppermute | solution.py:145

commit v2 on v0

v2 whole, which is shorter than its diff:
```python
import functools

import jax
import jax.numpy as jnp
from jax import lax
from jax.experimental import pallas as pl
from jax.experimental.pallas import tpu as pltpu
from jax.sharding import PartitionSpec as P

TILE = 64
ANY = pl.BlockSpec(memory_space=pl.ANY)
VMEM = pl.BlockSpec(memory_space=pltpu.VMEM)
SMEM = pl.BlockSpec(memory_space=pltpu.SMEM)


def near(array):
    return pltpu.with_memory_space_constraint(array, pltpu.VMEM)


def keep_present(mask_at, tiles_ref, out_ref):
    shape = (TILE, 2 * TILE)
    lane = lax.broadcasted_iota(jnp.int32, shape, 1)
    for i in range(tiles_ref.shape[0] // TILE):
        for j in range(0, tiles_ref.shape[1] // TILE, 2):
            place = (pl.ds(i * TILE, TILE), pl.ds(j * TILE, 2 * TILE))
            present = jnp.where(lane < TILE, mask_at(i, j), mask_at(i, j + 1)) != 0
            tiles = tiles_ref[place]
            out_ref[place] = jnp.where(present, tiles, jnp.zeros_like(tiles))


def mask_kernel(a_mask_ref, b_mask_ref, a_ref, b_ref, a_out_ref, b_out_ref):
    keep_present(lambda i, j: b_mask_ref[i, j], b_ref, b_out_ref)
    keep_present(lambda i, j: a_mask_ref[j, i], a_ref, a_out_ref)


def masked(a_tiles, a_mask, b_tiles, b_mask):
    return pl.pallas_call(
        mask_kernel,
        out_shape=(
            pltpu.VMEM(a_tiles.shape, a_tiles.dtype),
            pltpu.VMEM(b_tiles.shape, b_tiles.dtype),
        ),
        in_specs=[SMEM, SMEM, VMEM, VMEM],
        out_specs=(VMEM, VMEM),
        cost_estimate=pl.CostEstimate(
            flops=a_tiles.size + b_tiles.size,
            bytes_accessed=4 * (a_tiles.size + b_tiles.size),
            transcendentals=0,
        ),
    )(a_mask.T, b_mask, a_tiles, b_tiles)


def spread(mask):
    shape = (mask.shape[1], mask.shape[1] * TILE)
    owner = lax.broadcasted_iota(jnp.int32, shape, 1) // TILE
    ones = (owner == lax.broadcasted_iota(jnp.int32, shape, 0)).astype(jnp.float32)
    return jnp.dot(mask, ones, preferred_element_type=jnp.float32)


def early_kernel(b_distances, mesh_sizes, *refs):
    row_count, col_count = mesh_sizes
    ratio = col_count // row_count
    a_refs, refs = refs[:4], refs[4:]
    b_refs, (total_ref, a_last_ref, a_all) = refs[: row_count - 1], refs[row_count - 1 :]
    me_row, me_col = lax.axis_index("row"), lax.axis_index("col")
    width = a_all.shape[1] // col_count
    depth = ratio * width

    for distance in range(col_count):
        far, chip = divmod(distance // 2, col_count // 4)
        a_ref = a_refs[distance % 2 * 2 + far]
        block = pl.ds(chip * width, width)
        shift = (me_col ^ distance) - me_col
        stored = lax.rem(shift + ratio * me_row + ratio - 1 + 2 * col_count, col_count)
        a_all[:, pl.ds(pl.multiple_of(stored * width, width), width)] = a_ref[:, block]

    def a_columns(distance):
        return pl.ds(pl.multiple_of((me_row ^ distance) * depth, depth), depth)

    *distances, last = b_distances(me_col)
    a_last_ref[...] = a_all[:, a_columns(last)]
    for start in range(0, total_ref.shape[0], 2 * TILE):
        rows = pl.ds(start, 2 * TILE)
        total = None
        for distance, b_ref in zip(distances, b_refs, strict=True):
            term = jnp.dot(
                a_all[rows, a_columns(distance)], b_ref[...], preferred_element_type=jnp.float32
            )
            total = term if total is None else total + term
        total_ref[rows, :] = total


def early_product(a_blocks, b_blocks, b_distances, mesh_sizes):
    a_rows, half = a_blocks[0].shape
    depth, columns = b_blocks[0].shape
    inner = 4 * half
    return pl.pallas_call(
        functools.partial(early_kernel, b_distances, mesh_sizes),
        out_shape=(
            pltpu.VMEM((a_rows, columns), jnp.float32),
            pltpu.VMEM((a_rows, depth), jnp.bfloat16),
        ),
        in_specs=[VMEM] * (len(a_blocks) + len(b_blocks)),
        out_specs=(VMEM, VMEM),
        scratch_shapes=[pltpu.VMEM((a_rows, inner), jnp.bfloat16)],
        compiler_params=pltpu.CompilerParams(vmem_limit_bytes=24 * 1024 * 1024),
        cost_estimate=pl.CostEstimate(
            flops=2 * a_rows * (inner - depth) * columns,
            bytes_accessed=2 * (a_rows * inner + (inner - depth) * columns) + 4 * a_rows * columns,
            transcendentals=0,
        ),
    )(*(near(block) for block in (*a_blocks, *b_blocks)))


def last_kernel(row_ids_ref, c_keep_ref, total_ref, a_ref, b_ref, out_ref, out_tiles, out_sem):
    ids = row_ids_ref[...]
    which = lax.broadcasted_iota(jnp.int32, (ids.shape[0], c_keep_ref.shape[1]), 1)
    keep = spread(
        lax.dot_general(
            (ids == which).astype(jnp.float32),
            c_keep_ref[...].astype(jnp.float32),
            (((1,), (1,)), ((), ())),
            preferred_element_type=jnp.float32,
        )
    )
    rows = out_tiles.shape[1]
    writes = []
    for step in range(out_tiles.shape[0]):
        own = pl.ds(step * rows, rows)
        total = total_ref[own, :] + jnp.dot(
            a_ref[own, :], b_ref[...], preferred_element_type=jnp.float32
        )
        for i in range(rows // TILE):
            slot = step * rows // TILE + i
            out_tiles[step, pl.ds(i * TILE, TILE), :] = (
                total[i * TILE : (i + 1) * TILE] * keep[slot : slot + 1]
            ).astype(jnp.bfloat16)
        writes.append(pltpu.make_async_copy(out_tiles.at[step], out_ref.at[own, :], out_sem.at[step]))
        writes[-1].start()
    for write in writes:
        write.wait()


def last_product(row_ids, c_keep, total, a_last, b_last):
    a_rows, columns = total.shape
    rows = 2 * TILE
    steps = a_rows // rows
    return pl.pallas_call(
        last_kernel,
        out_shape=jax.ShapeDtypeStruct((a_rows, columns), jnp.bfloat16),
        in_specs=[VMEM] * 5,
        out_specs=ANY,
        scratch_shapes=[
            pltpu.VMEM((steps, rows, columns), jnp.bfloat16),
            pltpu.SemaphoreType.DMA((steps,)),
        ],
        compiler_params=pltpu.CompilerParams(vmem_limit_bytes=24 * 1024 * 1024),
        cost_estimate=pl.CostEstimate(
            flops=2 * a_rows * b_last.size,
            bytes_accessed=4 * total.size + 2 * (a_last.size + b_last.size + total.size),
            transcendentals=0,
        ),
    )(near(row_ids[:, None]), near(c_keep.T), near(total), near(a_last), near(b_last))


def swapped(block, axis, distance):
    return lax.ppermute(block, axis, [(i, i ^ distance) for i in range(lax.axis_size(axis))])


def crossed(block, even, odd):
    cols = lax.axis_size("col")
    pairs = [
        (r * cols + c, (r ^ (odd if c % 2 else even)) * cols + c)
        for r in range(lax.axis_size("row"))
        for c in range(cols)
    ]
    return lax.ppermute(block, ("row", "col"), pairs)


def gathered_b(b_eff):
    rows = lax.axis_size("row")
    if rows != 4:
        blocks = [b_eff] + [swapped(b_eff, "row", d) for d in range(1, rows)]
        return blocks, lambda col: tuple(range(rows))
    first = crossed(b_eff, 1, 2)
    second = crossed(b_eff, 2, 1)
    last = crossed(first, 2, 1)
    return [b_eff, first, second, last], lambda col: (0, 1 + (col & 1), 2 - (col & 1), 3)


def beside_kernel(*refs):
    *block_refs, out_ref = refs
    width = block_refs[0].shape[1]
    for i, block_ref in enumerate(block_refs):
        out_ref[:, i * width : (i + 1) * width] = block_ref[...]


def beside(blocks):
    rows, width = blocks[0].shape
    return pl.pallas_call(
        beside_kernel,
        out_shape=pltpu.VMEM((rows, width * len(blocks)), blocks[0].dtype),
        in_specs=[VMEM] * len(blocks),
        out_specs=VMEM,
        compiler_params=pltpu.CompilerParams(vmem_limit_bytes=24 * 1024 * 1024),
        cost_estimate=pl.CostEstimate(
            flops=0, bytes_accessed=4 * rows * width * len(blocks), transcendentals=0
        ),
    )(*(near(block) for block in blocks))


def gathered_a(a_eff):
    chips = [a_eff] + [swapped(a_eff, "col", d) for d in range(2, lax.axis_size("col"), 2)]
    middle = len(chips) // 2
    owns = [beside(chips[:middle]), beside(chips[middle:])]
    return owns + [swapped(own, "col", 1) for own in owns]


def per_device(row_ids, a_tiles, a_mask, b_tiles, b_mask, c_keep):
    a_eff, b_eff = masked(a_tiles, a_mask, b_tiles, b_mask)
    b_blocks, b_distances = gathered_b(b_eff)
    sizes = (lax.axis_size("row"), lax.axis_size("col"))
    total, a_last = early_product(gathered_a(a_eff), b_blocks[:-1], b_distances, sizes)
    return last_product(row_ids, c_keep, total, a_last, b_blocks[-1])


def solution(mesh):
    placed = (
        P("row"),
        P("row", "col"),
        P("row", "col"),
        P("row", "col"),
        P("row", "col"),
        P(None, "col"),
    )
    return jax.shard_map(
        per_device, mesh=mesh, in_specs=placed, out_specs=P("row", "col"), check_vma=False
    )
```

time: 70.6 us -> 22.2 us (0.31)
  the two profiles are of different devices: /device:TPU:0 before, /device:TPU:19 now
where the time goes in v2:
time: 22.2 us; the launch traced here: 22.1 us
  waiting for transfers between devices  12.2 us (55%)
  starting transfers between devices  6 us (27%)
  Pallas kernels  3.77 us (17%)
    ppermute x5, waiting for transfers between devices, swapped(): lax.ppermute(block, axis, [(i, i ^ distance) for i in range(lax.axis_size...  10.3 us
    ppermute x5, starting transfers between devices, swapped(): lax.ppermute(block, axis, [(i, i ^ distance) for i in range(lax.axis_size...  4.19 us
    ppermute x3, waiting for transfers between devices, crossed(): return lax.ppermute(block, ('row', 'col'), pairs)  1.88 us
    ppermute x3, starting transfers between devices, crossed(): return lax.ppermute(block, ('row', 'col'), pairs)  1.81 us
    pallas_call x1, Pallas kernels, last_product(): pl.pallas_call(last_kernel, out_shape=jax.ShapeDtypeStruct((a_rows, colum...  1.34 us
    pallas_call x1, Pallas kernels, masked(): pl.pallas_call(mask_kernel, out_shape=(pltpu.VMEM(a_tiles.shape, a_tiles....  1.21 us
    pallas_call x1, Pallas kernels, early_product(): pl.pallas_call(functools.partial(early_kernel, b_distances, mesh_sizes),...  1.13 us
  transfers between devices with their start and end apart: 8, of which 5 were waited for; matrix products, arithmetic and copies ran while one was open for 0% of the time, Pallas kernels for 6%

profile of v2, /device:TPU:19, one launch (start us, length us, event | category | flops | bytes accessed | tf_op | source)
XLA Modules:
  0.0 22.1 jit_solution(2500523043929151191)
XLA Ops:
  0.0 0.0 copy-start.1
  0.0 1.2 %shard_map.64 = (bf16[512,128]{1,0:T(8,128)(2,1)S(1)}, bf16[256,768]{1,0:T(8,128)(2,1)S(1)}) custom-call(s32[2,8]{1,0:T(2,128)} %bitcast.4, s32[4,12]{1,0:T(4,128)} %b_mask_ref.1, bf16[512,128]{1,0:T(8,128)(2,1)} %a_ref.1, bf16[256,768]{1,0:T(8,128)(2,1)} %b_ref.1), custom_call_target="tpu_custom_call" | custom-call | flops 262144 | bytes 1048576 | tf_op jit(solution)/shard_map/pallas_call | solution.py:37
  1.2 1.3 %collective-permute-start.5 = (bf16[256,768]{1,0:T(8,128)(2,1)S(1)}, bf16[256,768]{1,0:T(8,128)(2,1)S(1)}, u32[]{:S(2)}, u32[]{:S(2)}) collective-permute-start(bf16[256,768]{1,0:T(8,128)(2,1)S(1)} %get-tuple-element.10.refs_4_), channel_id=1, source_target_pairs={{0,8},{1,17},{2,10},{3,19},{4,12},{5,21},{6,14},{7,23},{8,0},{9,25... | collective-permute-start | bytes 1179656 | tf_op jit(solution)/shard_map/ppermute | solution.py:177
  2.5 0.0 copy-start
  2.5 0.1 collective-permute-start.1
  2.6 2.4 %collective-permute-start.2 = (bf16[512,128]{1,0:T(8,128)(2,1)S(1)}, bf16[512,128]{1,0:T(8,128)(2,1)S(1)}, u32[]{:S(2)}, u32[]{:S(2)}) collective-permute-start(bf16[512,128]{1,0:T(8,128)(2,1)S(1)} %get-tuple-element.9.refs_0_), channel_id=1, source_target_pairs={{0,6},{1,7},{2,4},{3,5},{4,2},{5,3},{6,0},{7,1},{8,14},{9,15},{10,... | collective-permute-start | bytes 393224 | tf_op jit(solution)/shard_map/ppermute | solution.py:167
  5.0 1.1 %collective-permute-start = (bf16[512,128]{1,0:T(8,128)(2,1)S(1)}, bf16[512,128]{1,0:T(8,128)(2,1)S(1)}, u32[]{:S(2)}, u32[]{:S(2)}) collective-permute-start(bf16[512,128]{1,0:T(8,128)(2,1)S(1)} %get-tuple-element.9.refs_0_), channel_id=1, source_target_pairs={{0,2},{1,3},{2,0},{3,1},{4,6},{5,7},{6,4},{7,5},{8,10},{9,11},{10,... | collective-permute-start | bytes 393224 | tf_op jit(solution)/shard_map/ppermute | solution.py:167
  6.1 0.3 %collective-permute-start.6 = (bf16[256,768]{1,0:T(8,128)(2,1)S(1)}, bf16[256,768]{1,0:T(8,128)(2,1)S(1)}, u32[]{:S(2)}, u32[]{:S(2)}) collective-permute-start(bf16[256,768]{1,0:T(8,128)(2,1)S(1)} %get-tuple-element.10.refs_4_), channel_id=1, source_target_pairs={{0,16},{1,9},{2,18},{3,11},{4,20},{5,13},{6,22},{7,15},{8,24},{9,1... | collective-permute-start | bytes 1179656 | tf_op jit(solution)/shard_map/ppermute | solution.py:177
  6.3 1.9 %collective-permute-done.5.refs_5_ = bf16[256,768]{1,0:T(8,128)(2,1)S(1)} collective-permute-done((bf16[256,768]{1,0:T(8,128)(2,1)S(1)}, bf16[256,768]{1,0:T(8,128)(2,1)S(1)}, u32[]{:S(2)}, u32[]{:S(2)}) %collective-permute-start.5) | collective-permute-done | bytes 393248 | tf_op jit(solution)/shard_map/ppermute | solution.py:177
  8.2 0.3 %collective-permute-start.7 = (bf16[256,768]{1,0:T(8,128)(2,1)S(1)}, bf16[256,768]{1,0:T(8,128)(2,1)S(1)}, u32[]{:S(2)}, u32[]{:S(2)}) collective-permute-start(bf16[256,768]{1,0:T(8,128)(2,1)S(1)} %collective-permute-done.5.refs_5_), channel_id=1, source_target_pairs={{0,16},{1,9},{2,18},{3,11},{4,20},{5,13},{6,22},{7,15},{8,24},{9,1... | collective-permute-start | bytes 1179656 | tf_op jit(solution)/shard_map/ppermute | solution.py:177
  8.5 3.0 %collective-permute-done.1.refs_0_ = bf16[512,128]{1,0:T(8,128)(2,1)S(1)} collective-permute-done((bf16[512,128]{1,0:T(8,128)(2,1)S(1)}, bf16[512,128]{1,0:T(8,128)(2,1)S(1)}, u32[]{:S(2)}, u32[]{:S(2)}) %collective-permute-start.1) | collective-permute-done | bytes 131104 | tf_op jit(solution)/shard_map/ppermute | solution.py:167
  11.5 5.9 %collective-permute-done.2.refs_1_ = bf16[512,128]{1,0:T(8,128)(2,1)S(1)} collective-permute-done((bf16[512,128]{1,0:T(8,128)(2,1)S(1)}, bf16[512,128]{1,0:T(8,128)(2,1)S(1)}, u32[]{:S(2)}, u32[]{:S(2)}) %collective-permute-start.2) | collective-permute-done | bytes 131104 | tf_op jit(solution)/shard_map/ppermute | solution.py:167
  17.4 0.5 %collective-permute-start.4 = (bf16[512,256]{1,0:T(8,128)(2,1)S(1)}, bf16[512,256]{1,0:T(8,128)(2,1)S(1)}, u32[]{:S(2)}, u32[]{:S(2)}) collective-permute-start(bf16[512,256]{1,0:T(8,128)(2,1)S(1)} %shard_map.66.refs_1_), channel_id=1, source_target_pairs={{0,1},{1,0},{2,3},{3,2},{4,5},{5,4},{6,7},{7,6},{8,9},{9,8},{10,11... | collective-permute-start | bytes 786440 | tf_op jit(solution)/shard_map/ppermute | solution.py:167
  17.9 0.0 collective-permute-done.refs_1_
  18.0 0.1 collective-permute-start.3
  18.1 0.0 copy-done.1
  18.1 0.1 copy.7.row_ids_ref
  18.2 0.9 %collective-permute-done.4.refs_3_ = bf16[512,256]{1,0:T(8,128)(2,1)S(1)} collective-permute-done((bf16[512,256]{1,0:T(8,128)(2,1)S(1)}, bf16[512,256]{1,0:T(8,128)(2,1)S(1)}, u32[]{:S(2)}, u32[]{:S(2)}) %collective-permute-start.4) | collective-permute-done | bytes 262176 | tf_op jit(solution)/shard_map/ppermute | solution.py:167
  19.1 0.5 %collective-permute-done.3.refs_2_ = bf16[512,256]{1,0:T(8,128)(2,1)S(1)} collective-permute-done((bf16[512,256]{1,0:T(8,128)(2,1)S(1)}, bf16[512,256]{1,0:T(8,128)(2,1)S(1)}, u32[]{:S(2)}, u32[]{:S(2)}) %collective-permute-start.3) | collective-permute-done | bytes 262176 | tf_op jit(solution)/shard_map/ppermute | solution.py:167
  19.6 0.0 collective-permute-done.6.refs_6_
  19.6 1.1 %shard_map.67 = (f32[512,768]{1,0:T(8,128)S(1)}, bf16[512,256]{1,0:T(8,128)(2,1)S(1)}) custom-call(bf16[512,256]{1,0:T(8,128)(2,1)S(1)} %shard_map.65.refs_0_, bf16[512,256]{1,0:T(8,128)(2,1)S(1)} %shard_map.66.refs_1_, bf16[512,256]{1,0:T(8,128)(2,1)S(1)} %collective-permute-done.3.refs_2_, bf16[512,256]{1,0:T(8,128)(2,1)S(1)} %collective-permute-done.4.refs_3_, ...), custom_call_target="tpu_custom_call" | custom-call | flops 603979776 | bytes 3801088 | tf_op jit(solution)/shard_map/pallas_call | solution.py:97
  20.7 0.0 collective-permute-done.7.b_ref
  20.7 0.0 copy-done
  20.7 1.3 %shard_map.68 = bf16[512,768]{1,0:T(8,128)(2,1)} custom-call(s32[8,1]{1,0:T(8,128)S(1)} %copy.7.row_ids_ref, s32[12,32]{1,0:T(8,128)S(1)} %bitcast.3, f32[512,768]{1,0:T(8,128)S(1)} %get-tuple-element.11.total_ref, bf16[512,256]{1,0:T(8,128)(2,1)S(1)} %get-tuple-element.12.a_ref, bf16[256,768]{1,0:T(8,128)(2,1)S(1)} %collective-permute-done.7.b_ref), custom_call_target="tpu_custom_call" | custom-call | flops 201326592 | bytes 3014656 | tf_op jit(solution)/shard_map/pallas_call | solution.py:148
  (2 shorter events, 0.1 us)
Async XLA Ops:
  0.0 18.1 %copy-start.1 = (s32[8]{0:T(128)S(1)}, s32[8]{0:T(128)}, u32[]{:S(2)}) copy-start(s32[8]{0:T(128)} %param.6) | copy-start | bytes 100
  1.2 7.0 %collective-permute-start.5 = (bf16[256,768]{1,0:T(8,128)(2,1)S(1)}, bf16[256,768]{1,0:T(8,128)(2,1)S(1)}, u32[]{:S(2)}, u32[]{:S(2)}) collective-permute-start(bf16[256,768]{1,0:T(8,128)(2,1)S(1)} %get-tuple-element.10.refs_4_), channel_id=1, source_target_pairs={{0,8},{1,17},{2,10},{3,19},{4,12},{5,21},{6,14},{7,23},{8,0},{9,25... | collective-permute-start | bytes 1179656 | tf_op jit(solution)/shard_map/ppermute | solution.py:177
  2.5 18.2 %copy-start = (s32[32,12]{0,1:T(8,128)S(1)}, s32[32,12]{0,1:T(8,128)}, u32[]{:S(2)}) copy-start(s32[32,12]{0,1:T(8,128)} %param.11) | copy-start | bytes 4612
  2.5 8.9 %collective-permute-start.1 = (bf16[512,128]{1,0:T(8,128)(2,1)S(1)}, bf16[512,128]{1,0:T(8,128)(2,1)S(1)}, u32[]{:S(2)}, u32[]{:S(2)}) collective-permute-start(bf16[512,128]{1,0:T(8,128)(2,1)S(1)} %get-tuple-element.9.refs_0_), channel_id=1, source_target_pairs={{0,4},{1,5},{2,6},{3,7},{4,0},{5,1},{6,2},{7,3},{8,12},{9,13},{10,... | collective-permute-start | bytes 393224 | tf_op jit(solution)/shard_map/ppermute | solution.py:167
  2.6 14.8 %collective-permute-start.2 = (bf16[512,128]{1,0:T(8,128)(2,1)S(1)}, bf16[512,128]{1,0:T(8,128)(2,1)S(1)}, u32[]{:S(2)}, u32[]{:S(2)}) collective-permute-start(bf16[512,128]{1,0:T(8,128)(2,1)S(1)} %get-tuple-element.9.refs_0_), channel_id=1, source_target_pairs={{0,6},{1,7},{2,4},{3,5},{4,2},{5,3},{6,0},{7,1},{8,14},{9,15},{10,... | collective-permute-start | bytes 393224 | tf_op jit(solution)/shard_map/ppermute | solution.py:167
  5.0 12.9 %collective-permute-start = (bf16[512,128]{1,0:T(8,128)(2,1)S(1)}, bf16[512,128]{1,0:T(8,128)(2,1)S(1)}, u32[]{:S(2)}, u32[]{:S(2)}) collective-permute-start(bf16[512,128]{1,0:T(8,128)(2,1)S(1)} %get-tuple-element.9.refs_0_), channel_id=1, source_target_pairs={{0,2},{1,3},{2,0},{3,1},{4,6},{5,7},{6,4},{7,5},{8,10},{9,11},{10,... | collective-permute-start | bytes 393224 | tf_op jit(solution)/shard_map/ppermute | solution.py:167
  6.1 13.5 %collective-permute-start.6 = (bf16[256,768]{1,0:T(8,128)(2,1)S(1)}, bf16[256,768]{1,0:T(8,128)(2,1)S(1)}, u32[]{:S(2)}, u32[]{:S(2)}) collective-permute-start(bf16[256,768]{1,0:T(8,128)(2,1)S(1)} %get-tuple-element.10.refs_4_), channel_id=1, source_target_pairs={{0,16},{1,9},{2,18},{3,11},{4,20},{5,13},{6,22},{7,15},{8,24},{9,1... | collective-permute-start | bytes 1179656 | tf_op jit(solution)/shard_map/ppermute | solution.py:177
  8.2 12.5 %collective-permute-start.7 = (bf16[256,768]{1,0:T(8,128)(2,1)S(1)}, bf16[256,768]{1,0:T(8,128)(2,1)S(1)}, u32[]{:S(2)}, u32[]{:S(2)}) collective-permute-start(bf16[256,768]{1,0:T(8,128)(2,1)S(1)} %collective-permute-done.5.refs_5_), channel_id=1, source_target_pairs={{0,16},{1,9},{2,18},{3,11},{4,20},{5,13},{6,22},{7,15},{8,24},{9,1... | collective-permute-start | bytes 1179656 | tf_op jit(solution)/shard_map/ppermute | solution.py:177
  17.4 1.7 %collective-permute-start.4 = (bf16[512,256]{1,0:T(8,128)(2,1)S(1)}, bf16[512,256]{1,0:T(8,128)(2,1)S(1)}, u32[]{:S(2)}, u32[]{:S(2)}) collective-permute-start(bf16[512,256]{1,0:T(8,128)(2,1)S(1)} %shard_map.66.refs_1_), channel_id=1, source_target_pairs={{0,1},{1,0},{2,3},{3,2},{4,5},{5,4},{6,7},{7,6},{8,9},{9,8},{10,11... | collective-permute-start | bytes 786440 | tf_op jit(solution)/shard_map/ppermute | solution.py:167
  18.0 1.6 %collective-permute-start.3 = (bf16[512,256]{1,0:T(8,128)(2,1)S(1)}, bf16[512,256]{1,0:T(8,128)(2,1)S(1)}, u32[]{:S(2)}, u32[]{:S(2)}) collective-permute-start(bf16[512,256]{1,0:T(8,128)(2,1)S(1)} %shard_map.65.refs_0_), channel_id=1, source_target_pairs={{0,1},{1,0},{2,3},{3,2},{4,5},{5,4},{6,7},{7,6},{8,9},{9,8},{10,11... | collective-permute-start | bytes 786440 | tf_op jit(solution)/shard_map/ppermute | solution.py:167

commit v3 on v2

v3 whole, which is shorter than its diff:
```python
import functools

import jax
import jax.numpy as jnp
from jax import lax
from jax.experimental import pallas as pl
from jax.experimental.pallas import tpu as pltpu
from jax.sharding import PartitionSpec as P

TILE = 64
ANY = pl.BlockSpec(memory_space=pl.ANY)
VMEM = pl.BlockSpec(memory_space=pltpu.VMEM)
SMEM = pl.BlockSpec(memory_space=pltpu.SMEM)
LIMITS = pltpu.CompilerParams(vmem_limit_bytes=24 * 1024 * 1024)


def near(array):
    return pltpu.with_memory_space_constraint(array, pltpu.VMEM)


def cost(flops, bytes_accessed):
    return pl.CostEstimate(flops=flops, bytes_accessed=bytes_accessed, transcendentals=0)


def keep_present(mask_at, tiles_ref, out_ref):
    lane = lax.broadcasted_iota(jnp.int32, (TILE, 2 * TILE), 1)
    for i in range(tiles_ref.shape[0] // TILE):
        for j in range(0, tiles_ref.shape[1] // TILE, 2):
            place = (pl.ds(i * TILE, TILE), pl.ds(j * TILE, 2 * TILE))
            present = jnp.where(lane < TILE, mask_at(i, j), mask_at(i, j + 1)) != 0
            tiles = tiles_ref[place]
            out_ref[place] = jnp.where(present, tiles, jnp.zeros_like(tiles))


def mask_kernel(a_mask_ref, b_mask_ref, a_ref, b_ref, a_out_ref, b_out_ref):
    keep_present(lambda i, j: b_mask_ref[i, j], b_ref, b_out_ref)
    keep_present(lambda i, j: a_mask_ref[j, i], a_ref, a_out_ref)


def masked(a_tiles, a_mask, b_tiles, b_mask):
    size = a_tiles.size + b_tiles.size
    return pl.pallas_call(
        mask_kernel,
        out_shape=(
            pltpu.VMEM(a_tiles.shape, a_tiles.dtype),
            pltpu.VMEM(b_tiles.shape, b_tiles.dtype),
        ),
        in_specs=[SMEM, SMEM, VMEM, VMEM],
        out_specs=(VMEM, VMEM),
        cost_estimate=cost(size, 4 * size),
    )(a_mask.T, b_mask, a_tiles, b_tiles)


def spread(mask):
    shape = (mask.shape[1], mask.shape[1] * TILE)
    owner = lax.broadcasted_iota(jnp.int32, shape, 1) // TILE
    ones = (owner == lax.broadcasted_iota(jnp.int32, shape, 0)).astype(jnp.float32)
    return jnp.dot(mask, ones, preferred_element_type=jnp.float32)


def put_in_order(b_place, mesh_sizes, width, groups, panels_ref):
    row_count, col_count = mesh_sizes
    ratio = col_count // row_count
    me_row, me_col = lax.axis_index("row"), lax.axis_index("col")
    for array_ref, distances in groups:
        for i, distance in enumerate(distances):
            shift = (me_col ^ distance) - me_col
            stored = lax.rem(shift + ratio * me_row + ratio - 1 + 2 * col_count, col_count)
            place = b_place((stored // ratio) ^ me_row)
            columns = pl.ds(pl.multiple_of(place * width, width), width)
            panels_ref[:, columns] = array_ref[:, i * width : (i + 1) * width]


def early_kernel(distances, b_place, mesh_sizes, row_ids_ref, c_keep_ref, *refs):
    a_refs, refs = refs[: len(distances)], refs[len(distances) :]
    early = mesh_sizes[0] - 1
    b_refs, (total_ref, a_last_ref, keep_ref, panels) = refs[:early], refs[early:]
    width = a_last_ref.shape[1]
    put_in_order(b_place, mesh_sizes, width, zip(a_refs, distances, strict=True), panels)
    a_last_ref[...] = panels[:, early * width :]
    second = jnp.concatenate([b_ref[width:, :] for b_ref in b_refs], axis=0)
    for start in range(0, total_ref.shape[0], 2 * TILE):
        rows = pl.ds(start, 2 * TILE)
        total_ref[rows, :] = jnp.dot(
            panels[rows, : early * width], second, preferred_element_type=jnp.float32
        )
    ids = row_ids_ref[...]
    which = lax.broadcasted_iota(jnp.int32, (ids.shape[0], c_keep_ref.shape[1]), 1)
    keep_ref[...] = spread(
        lax.dot_general(
            (ids == which).astype(jnp.float32),
            c_keep_ref[...].astype(jnp.float32),
            (((1,), (1,)), ((), ())),
            preferred_element_type=jnp.float32,
        )
    )


def early_product(row_ids, c_keep, a_groups, b_blocks, b_place, mesh_sizes):
    arrays, distances = zip(*a_groups, strict=True)
    a_rows = arrays[0].shape[0]
    depth, columns = b_blocks[0].shape
    width = depth // 2
    return pl.pallas_call(
        functools.partial(early_kernel, distances, b_place, mesh_sizes),
        out_shape=(
            pltpu.VMEM((a_rows, columns), jnp.float32),
            pltpu.VMEM((a_rows, width), jnp.bfloat16),
            pltpu.VMEM((row_ids.shape[0], columns), jnp.float32),
        ),
        in_specs=[VMEM] * (2 + len(arrays) + len(b_blocks)),
        out_specs=(VMEM, VMEM, VMEM),
        scratch_shapes=[pltpu.VMEM((a_rows, width * mesh_sizes[0]), jnp.bfloat16)],
        compiler_params=LIMITS,
        cost_estimate=cost(2 * a_rows * width * len(b_blocks) * columns, 4 * a_rows * columns),
    )(near(row_ids[:, None]), near(c_keep.T), *(near(block) for block in (*arrays, *b_blocks)))


def last_kernel(distances, b_place, mesh_sizes, keep_ref, total_ref, a_last_ref, *refs):
    row_count = mesh_sizes[0]
    a_refs, refs = refs[: len(distances)], refs[len(distances) :]
    b_refs, (out_ref, panels, out_tiles, out_sem) = refs[:row_count], refs[row_count:]
    width = a_last_ref.shape[1]
    put_in_order(b_place, mesh_sizes, width, zip(a_refs, distances, strict=True), panels)
    panels[:, row_count * width :] = a_last_ref[...]
    blocks = jnp.concatenate(
        [b_ref[:width, :] for b_ref in b_refs] + [b_refs[-1][width:, :]], axis=0
    )
    rows = out_tiles.shape[1]
    writes = []
    for step in range(out_tiles.shape[0]):
        own = pl.ds(step * rows, rows)
        total = total_ref[own, :] + jnp.dot(
            panels[own, :], blocks, preferred_element_type=jnp.float32
        )
        for i in range(rows // TILE):
            slot = step * rows // TILE + i
            out_tiles[step, pl.ds(i * TILE, TILE), :] = (
                total[i * TILE : (i + 1) * TILE] * keep_ref[slot : slot + 1, :]
            ).astype(jnp.bfloat16)
        writes.append(
            pltpu.make_async_copy(out_tiles.at[step], out_ref.at[own, :], out_sem.at[step])
        )
        writes[-1].start()
    for write in writes:
        write.wait()


def last_product(keep, total, a_last, a_groups, b_blocks, b_place, mesh_sizes):
    arrays, distances = zip(*a_groups, strict=True)
    a_rows, columns = total.shape
    inner = a_last.shape[1] * (mesh_sizes[0] + 1)
    rows = 2 * TILE
    steps = a_rows // rows
    return pl.pallas_call(
        functools.partial(last_kernel, distances, b_place, mesh_sizes),
        out_shape=jax.ShapeDtypeStruct((a_rows, columns), jnp.bfloat16),
        in_specs=[VMEM] * (3 + len(arrays) + len(b_blocks)),
        out_specs=ANY,
        scratch_shapes=[
            pltpu.VMEM((a_rows, inner), jnp.bfloat16),
            pltpu.VMEM((steps, rows, columns), jnp.bfloat16),
            pltpu.SemaphoreType.DMA((steps,)),
        ],
        compiler_params=LIMITS,
        cost_estimate=cost(2 * a_rows * inner * columns, 6 * total.size),
    )(*(near(array) for array in (keep, total, a_last, *arrays, *b_blocks)))


def swapped(block, axis, distance):
    return lax.ppermute(block, axis, [(i, i ^ distance) for i in range(lax.axis_size(axis))])


def crossed(block, even, odd):
    cols = lax.axis_size("col")
    pairs = [
        (r * cols + c, (r ^ (odd if c % 2 else even)) * cols + c)
        for r in range(lax.axis_size("row"))
        for c in range(cols)
    ]
    return lax.ppermute(block, ("row", "col"), pairs)


def gathered_b(b_eff):
    rows = lax.axis_size("row")
    if rows != 4:
        return [b_eff] + [swapped(b_eff, "row", d) for d in range(1, rows)], lambda distance: distance
    first = crossed(b_eff, 1, 2)
    second = crossed(b_eff, 2, 1)
    last = crossed(first, 2, 1)

    def place(distance):
        odd = lax.axis_index("col") & 1
        return jnp.where((distance == 0) | (distance == 3), distance, distance ^ (3 * odd))

    return [b_eff, first, second, last], place


def beside_kernel(*refs):
    *block_refs, out_ref = refs
    width = block_refs[0].shape[1]
    for i, block_ref in enumerate(block_refs):
        out_ref[:, i * width : (i + 1) * width] = block_ref[...]


def beside(blocks):
    rows, width = blocks[0].shape
    return pl.pallas_call(
        beside_kernel,
        out_shape=pltpu.VMEM((rows, width * len(blocks)), blocks[0].dtype),
        in_specs=[VMEM] * len(blocks),
        out_specs=VMEM,
        compiler_params=LIMITS,
        cost_estimate=cost(0, 4 * rows * width * len(blocks)),
    )(*(near(block) for block in blocks))


def started_early(block):
    return pl.pallas_call(
        lambda block_ref, same_ref: None,
        out_shape=pltpu.VMEM(block.shape, block.dtype),
        in_specs=[VMEM],
        out_specs=VMEM,
        input_output_aliases={0: 0},
        cost_estimate=cost(460_000_000, 0),
    )(near(block))


def gathered_a(a_eff):
    cols = lax.axis_size("col")
    blocks = {0: a_eff} | {d: swapped(a_eff, "col", d) for d in range(2, cols, 2)}
    if cols == 8:
        blocks[6] = started_early(blocks[6])
        groups = ((0, 4), (2, 6))
    else:
        groups = (tuple(blocks)[: cols // 4], tuple(blocks)[cols // 4 :])
    owns = [(beside([blocks[d] for d in group]), group) for group in groups]
    partners = [(swapped(own, "col", 1), tuple(d ^ 1 for d in group)) for own, group in owns]
    return owns, partners


def per_device(row_ids, a_tiles, a_mask, b_tiles, b_mask, c_keep):
    sizes = (lax.axis_size("row"), lax.axis_size("col"))
    assert sizes[1] == 2 * sizes[0] and b_tiles.shape[0] == 2 * a_tiles.shape[1]
    a_eff, b_eff = masked(a_tiles, a_mask, b_tiles, b_mask)
    b_blocks, b_place = gathered_b(b_eff)
    owns, partners = gathered_a(a_eff)
    total, a_last, keep = early_product(row_ids, c_keep, owns, b_blocks[:-1], b_place, sizes)
    return last_product(keep, total, a_last, partners, b_blocks, b_place, sizes)


def solution(mesh):
    placed = (
        P("row"),
        P("row", "col"),
        P("row", "col"),
        P("row", "col"),
        P("row", "col"),
        P(None, "col"),
    )
    return jax.shard_map(
        per_device, mesh=mesh, in_specs=placed, out_specs=P("row", "col"), check_vma=False
    )
```

time: 22.2 us -> 21.9 us (0.986)
  the two profiles are of different devices: /device:TPU:19 before, /device:TPU:0 now
where the time goes in v3:
time: 21.9 us; the launch traced here: 21.8 us
  starting transfers between devices  12.4 us (57%)
  waiting for transfers between devices  5.56 us (25%)
  Pallas kernels  3.74 us (17%)
    ppermute x3, starting transfers between devices, crossed(): return lax.ppermute(block, ('row', 'col'), pairs)  8.04 us
    ppermute x5, waiting for transfers between devices, swapped(): lax.ppermute(block, axis, [(i, i ^ distance) for i in range(lax.axis_size...  4.86 us
    ppermute x5, starting transfers between devices, swapped(): lax.ppermute(block, axis, [(i, i ^ distance) for i in range(lax.axis_size...  4.31 us
    pallas_call x1, Pallas kernels, last_product(): pl.pallas_call(functools.partial(last_kernel, distances, b_place, mesh_si...  1.64 us
    pallas_call x1, Pallas kernels, masked(): pl.pallas_call(mask_kernel, out_shape=(pltpu.VMEM(a_tiles.shape, a_tiles....  1.22 us
    pallas_call x1, Pallas kernels, early_product(): pl.pallas_call(functools.partial(early_kernel, distances, b_place, mesh_s...  0.79 us
    ppermute x3, waiting for transfers between devices, crossed(): return lax.ppermute(block, ('row', 'col'), pairs)  0.7 us
  transfers between devices with their start and end apart: 8, of which 5 were waited for; matrix products, arithmetic and copies ran while one was open for 0% of the time, Pallas kernels for 4%

profile of v3, /device:TPU:0, one launch (start us, length us, event | category | flops | bytes accessed | tf_op | source)
XLA Modules:
  0.0 21.8 jit_solution(12865274148792688885)
XLA Ops:
  0.0 0.0 copy-start.1
  0.0 0.0 copy-start
  0.0 1.2 %shard_map.64 = (bf16[512,128]{1,0:T(8,128)(2,1)S(1)}, bf16[256,768]{1,0:T(8,128)(2,1)S(1)}) custom-call(s32[2,8]{1,0:T(2,128)} %bitcast.4, s32[4,12]{1,0:T(4,128)} %b_mask_ref.1, bf16[512,128]{1,0:T(8,128)(2,1)} %a_ref.1, bf16[256,768]{1,0:T(8,128)(2,1)} %b_ref.1), custom_call_target="tpu_custom_call" | custom-call | flops 262144 | bytes 1048576 | tf_op jit(solution)/shard_map/pallas_call | solution.py:42
  1.2 3.0 %collective-permute-start.3 = (bf16[256,768]{1,0:T(8,128)(2,1)S(1)}, bf16[256,768]{1,0:T(8,128)(2,1)S(1)}, u32[]{:S(2)}, u32[]{:S(2)}) collective-permute-start(bf16[256,768]{1,0:T(8,128)(2,1)S(1)} %get-tuple-element.11.refs_2_), channel_id=1, source_target_pairs={{0,8},{1,17},{2,10},{3,19},{4,12},{5,21},{6,14},{7,23},{8,0},{9,25... | collective-permute-start | bytes 1179656 | tf_op jit(solution)/shard_map/ppermute | solution.py:181
  4.2 2.6 %collective-permute-start = (bf16[512,128]{1,0:T(8,128)(2,1)S(1)}, bf16[512,128]{1,0:T(8,128)(2,1)S(1)}, u32[]{:S(2)}, u32[]{:S(2)}) collective-permute-start(bf16[512,128]{1,0:T(8,128)(2,1)S(1)} %get-tuple-element.10.refs_0_), channel_id=1, source_target_pairs={{0,4},{1,5},{2,6},{3,7},{4,0},{5,1},{6,2},{7,3},{8,12},{9,13},{10,... | collective-permute-start | bytes 393224 | tf_op jit(solution)/shard_map/ppermute | solution.py:171
  6.8 1.3 %collective-permute-start.2 = (bf16[512,128]{1,0:T(8,128)(2,1)S(1)}, bf16[512,128]{1,0:T(8,128)(2,1)S(1)}, u32[]{:S(2)}, u32[]{:S(2)}) collective-permute-start(bf16[512,128]{1,0:T(8,128)(2,1)S(1)} %get-tuple-element.10.refs_0_), channel_id=1, source_target_pairs={{0,6},{1,7},{2,4},{3,5},{4,2},{5,3},{6,0},{7,1},{8,14},{9,15},{10,... | collective-permute-start | bytes 393224 | tf_op jit(solution)/shard_map/ppermute | solution.py:171
  8.2 1.5 %collective-permute-start.4 = (bf16[256,768]{1,0:T(8,128)(2,1)S(1)}, bf16[256,768]{1,0:T(8,128)(2,1)S(1)}, u32[]{:S(2)}, u32[]{:S(2)}) collective-permute-start(bf16[256,768]{1,0:T(8,128)(2,1)S(1)} %get-tuple-element.11.refs_2_), channel_id=1, source_target_pairs={{0,16},{1,9},{2,18},{3,11},{4,20},{5,13},{6,22},{7,15},{8,24},{9,1... | collective-permute-start | bytes 1179656 | tf_op jit(solution)/shard_map/ppermute | solution.py:181
  9.7 0.2 %collective-permute-start.1 = (bf16[512,128]{1,0:T(8,128)(2,1)S(1)}, bf16[512,128]{1,0:T(8,128)(2,1)S(1)}, u32[]{:S(2)}, u32[]{:S(2)}) collective-permute-start(bf16[512,128]{1,0:T(8,128)(2,1)S(1)} %get-tuple-element.10.refs_0_), channel_id=1, source_target_pairs={{0,2},{1,3},{2,0},{3,1},{4,6},{5,7},{6,4},{7,5},{8,10},{9,11},{10,... | collective-permute-start | bytes 393224 | tf_op jit(solution)/shard_map/ppermute | solution.py:171
  9.9 0.3 %collective-permute-done.3.refs_3_ = bf16[256,768]{1,0:T(8,128)(2,1)S(1)} collective-permute-done((bf16[256,768]{1,0:T(8,128)(2,1)S(1)}, bf16[256,768]{1,0:T(8,128)(2,1)S(1)}, u32[]{:S(2)}, u32[]{:S(2)}) %collective-permute-start.3) | collective-permute-done | bytes 393248 | tf_op jit(solution)/shard_map/ppermute | solution.py:181
  10.2 3.5 %collective-permute-start.7 = (bf16[256,768]{1,0:T(8,128)(2,1)S(1)}, bf16[256,768]{1,0:T(8,128)(2,1)S(1)}, u32[]{:S(2)}, u32[]{:S(2)}) collective-permute-start(bf16[256,768]{1,0:T(8,128)(2,1)S(1)} %collective-permute-done.3.refs_3_), channel_id=1, source_target_pairs={{0,16},{1,9},{2,18},{3,11},{4,20},{5,13},{6,22},{7,15},{8,24},{9,1... | collective-permute-start | bytes 1179656 | tf_op jit(solution)/shard_map/ppermute | solution.py:181
  13.7 3.2 %collective-permute-done.refs_1_ = bf16[512,128]{1,0:T(8,128)(2,1)S(1)} collective-permute-done((bf16[512,128]{1,0:T(8,128)(2,1)S(1)}, bf16[512,128]{1,0:T(8,128)(2,1)S(1)}, u32[]{:S(2)}, u32[]{:S(2)}) %collective-permute-start) | collective-permute-done | bytes 131104 | tf_op jit(solution)/shard_map/ppermute | solution.py:171
  17.0 0.1 collective-permute-start.5
  17.1 0.0 collective-permute-done.2.block_ref
  17.1 1.0 %collective-permute-done.1.refs_0_ = bf16[512,128]{1,0:T(8,128)(2,1)S(1)} collective-permute-done((bf16[512,128]{1,0:T(8,128)(2,1)S(1)}, bf16[512,128]{1,0:T(8,128)(2,1)S(1)}, u32[]{:S(2)}, u32[]{:S(2)}) %collective-permute-start.1) | collective-permute-done | bytes 131104 | tf_op jit(solution)/shard_map/ppermute | solution.py:171
  18.1 0.1 collective-permute-start.6
  18.2 0.0 copy-done.1
  18.2 0.1 copy.8.row_ids_ref
  18.3 0.0 collective-permute-done.4.refs_4_
  18.3 0.0 copy-done
  18.3 0.8 %shard_map.68 = (f32[512,768]{1,0:T(8,128)S(1)}, bf16[512,128]{1,0:T(8,128)(2,1)S(1)}, f32[8,768]{1,0:T(8,128)S(1)}) custom-call(s32[8,1]{1,0:T(8,128)S(1)} %copy.8.row_ids_ref, s32[12,32]{1,0:T(8,128)S(1)} %bitcast.3, bf16[512,256]{1,0:T(8,128)(2,1)S(1)} %shard_map.65.refs_0_, bf16[512,256]{1,0:T(8,128)(2,1)S(1)} %shard_map.67.refs_1_, ...), custom_call_target="tpu_custom_call" | custom-call | flops 301989888 | bytes 1572864 | tf_op jit(solution)/shard_map/pallas_call | solution.py:104
  19.1 0.0 collective-permute-done.5.refs_0_
  19.1 0.6 %collective-permute-done.6.refs_1_ = bf16[512,256]{1,0:T(8,128)(2,1)S(1)} collective-permute-done((bf16[512,256]{1,0:T(8,128)(2,1)S(1)}, bf16[512,256]{1,0:T(8,128)(2,1)S(1)}, u32[]{:S(2)}, u32[]{:S(2)}) %collective-permute-start.6) | collective-permute-done | bytes 262176 | tf_op jit(solution)/shard_map/ppermute | solution.py:171
  19.7 0.4 %collective-permute-done.7.refs_5_ = bf16[256,768]{1,0:T(8,128)(2,1)S(1)} collective-permute-done((bf16[256,768]{1,0:T(8,128)(2,1)S(1)}, bf16[256,768]{1,0:T(8,128)(2,1)S(1)}, u32[]{:S(2)}, u32[]{:S(2)}) %collective-permute-start.7) | collective-permute-done | bytes 393248 | tf_op jit(solution)/shard_map/ppermute | solution.py:181
  20.2 1.6 %shard_map.69 = bf16[512,768]{1,0:T(8,128)(2,1)} custom-call(f32[8,768]{1,0:T(8,128)S(1)} %get-tuple-element.12.keep_ref, f32[512,768]{1,0:T(8,128)S(1)} %get-tuple-element.13.total_ref, bf16[512,128]{1,0:T(8,128)(2,1)S(1)} %get-tuple-element.14.a_last_ref, bf16[512,256]{1,0:T(8,128)(2,1)S(1)} %collective-permute-done.5.refs_0_, ...), custom_call_target="tpu_custom_call" | custom-call | flops 503316480 | bytes 2359296 | tf_op jit(solution)/shard_map/pallas_call | solution.py:155
  (3 shorter events, 0.1 us)
Async XLA Ops:
  0.0 18.2 %copy-start.1 = (s32[8]{0:T(128)S(1)}, s32[8]{0:T(128)}, u32[]{:S(2)}) copy-start(s32[8]{0:T(128)} %param.6) | copy-start | bytes 100
  0.0 18.3 %copy-start = (s32[32,12]{0,1:T(8,128)S(1)}, s32[32,12]{0,1:T(8,128)}, u32[]{:S(2)}) copy-start(s32[32,12]{0,1:T(8,128)} %param.11) | copy-start | bytes 4612
  1.2 9.0 %collective-permute-start.3 = (bf16[256,768]{1,0:T(8,128)(2,1)S(1)}, bf16[256,768]{1,0:T(8,128)(2,1)S(1)}, u32[]{:S(2)}, u32[]{:S(2)}) collective-permute-start(bf16[256,768]{1,0:T(8,128)(2,1)S(1)} %get-tuple-element.11.refs_2_), channel_id=1, source_target_pairs={{0,8},{1,17},{2,10},{3,19},{4,12},{5,21},{6,14},{7,23},{8,0},{9,25... | collective-permute-start | bytes 1179656 | tf_op jit(solution)/shard_map/ppermute | solution.py:181
  4.2 12.7 %collective-permute-start = (bf16[512,128]{1,0:T(8,128)(2,1)S(1)}, bf16[512,128]{1,0:T(8,128)(2,1)S(1)}, u32[]{:S(2)}, u32[]{:S(2)}) collective-permute-start(bf16[512,128]{1,0:T(8,128)(2,1)S(1)} %get-tuple-element.10.refs_0_), channel_id=1, source_target_pairs={{0,4},{1,5},{2,6},{3,7},{4,0},{5,1},{6,2},{7,3},{8,12},{9,13},{10,... | collective-permute-start | bytes 393224 | tf_op jit(solution)/shard_map/ppermute | solution.py:171
  6.8 10.2 %collective-permute-start.2 = (bf16[512,128]{1,0:T(8,128)(2,1)S(1)}, bf16[512,128]{1,0:T(8,128)(2,1)S(1)}, u32[]{:S(2)}, u32[]{:S(2)}) collective-permute-start(bf16[512,128]{1,0:T(8,128)(2,1)S(1)} %get-tuple-element.10.refs_0_), channel_id=1, source_target_pairs={{0,6},{1,7},{2,4},{3,5},{4,2},{5,3},{6,0},{7,1},{8,14},{9,15},{10,... | collective-permute-start | bytes 393224 | tf_op jit(solution)/shard_map/ppermute | solution.py:171
  8.2 10.1 %collective-permute-start.4 = (bf16[256,768]{1,0:T(8,128)(2,1)S(1)}, bf16[256,768]{1,0:T(8,128)(2,1)S(1)}, u32[]{:S(2)}, u32[]{:S(2)}) collective-permute-start(bf16[256,768]{1,0:T(8,128)(2,1)S(1)} %get-tuple-element.11.refs_2_), channel_id=1, source_target_pairs={{0,16},{1,9},{2,18},{3,11},{4,20},{5,13},{6,22},{7,15},{8,24},{9,1... | collective-permute-start | bytes 1179656 | tf_op jit(solution)/shard_map/ppermute | solution.py:181
  9.7 8.4 %collective-permute-start.1 = (bf16[512,128]{1,0:T(8,128)(2,1)S(1)}, bf16[512,128]{1,0:T(8,128)(2,1)S(1)}, u32[]{:S(2)}, u32[]{:S(2)}) collective-permute-start(bf16[512,128]{1,0:T(8,128)(2,1)S(1)} %get-tuple-element.10.refs_0_), channel_id=1, source_target_pairs={{0,2},{1,3},{2,0},{3,1},{4,6},{5,7},{6,4},{7,5},{8,10},{9,11},{10,... | collective-permute-start | bytes 393224 | tf_op jit(solution)/shard_map/ppermute | solution.py:171
  10.2 10.0 %collective-permute-start.7 = (bf16[256,768]{1,0:T(8,128)(2,1)S(1)}, bf16[256,768]{1,0:T(8,128)(2,1)S(1)}, u32[]{:S(2)}, u32[]{:S(2)}) collective-permute-start(bf16[256,768]{1,0:T(8,128)(2,1)S(1)} %collective-permute-done.3.refs_3_), channel_id=1, source_target_pairs={{0,16},{1,9},{2,18},{3,11},{4,20},{5,13},{6,22},{7,15},{8,24},{9,1... | collective-permute-start | bytes 1179656 | tf_op jit(solution)/shard_map/ppermute | solution.py:181
  17.0 2.1 %collective-permute-start.5 = (bf16[512,256]{1,0:T(8,128)(2,1)S(1)}, bf16[512,256]{1,0:T(8,128)(2,1)S(1)}, u32[]{:S(2)}, u32[]{:S(2)}) collective-permute-start(bf16[512,256]{1,0:T(8,128)(2,1)S(1)} %shard_map.65.refs_0_), channel_id=1, source_target_pairs={{0,1},{1,0},{2,3},{3,2},{4,5},{5,4},{6,7},{7,6},{8,9},{9,8},{10,11... | collective-permute-start | bytes 786440 | tf_op jit(solution)/shard_map/ppermute | solution.py:171
  18.1 1.6 %collective-permute-start.6 = (bf16[512,256]{1,0:T(8,128)(2,1)S(1)}, bf16[512,256]{1,0:T(8,128)(2,1)S(1)}, u32[]{:S(2)}, u32[]{:S(2)}) collective-permute-start(bf16[512,256]{1,0:T(8,128)(2,1)S(1)} %shard_map.67.refs_1_), channel_id=1, source_target_pairs={{0,1},{1,0},{2,3},{3,2},{4,5},{5,4},{6,7},{7,6},{8,9},{9,8},{10,11... | collective-permute-start | bytes 786440 | tf_op jit(solution)/shard_map/ppermute | solution.py:171

commit v4 on v3

--- a/solution.py
+++ b/solution.py
@@ -58,31 +58,47 @@
     return jnp.dot(mask, ones, preferred_element_type=jnp.float32)
 
 
-def put_in_order(b_place, mesh_sizes, width, groups, panels_ref):
+def met_by(distance, b_place, mesh_sizes):
     row_count, col_count = mesh_sizes
     ratio = col_count // row_count
     me_row, me_col = lax.axis_index("row"), lax.axis_index("col")
-    for array_ref, distances in groups:
+    shift = (me_col ^ distance) - me_col
+    stored = lax.rem(shift + ratio * me_row + ratio - 1 + 2 * col_count, col_count)
+    return b_place((stored // ratio) ^ me_row)
+
+
+def early_kernel(own_distances, partner_distances, b_place, mesh_sizes, row_ids_ref, c_keep_ref, *refs):
+    row_count = mesh_sizes[0]
+    early = row_count - 1
+    own_refs, refs = refs[: len(own_distances)], refs[len(own_distances) :]
+    partner_ref, *refs = refs
+    b_refs, (total_ref, tail_ref, keep_ref, firsts_ref, panels) = refs[:early], refs[early:]
+    width = b_refs[0].shape[0] // 2
+
+    def put(block, distance, side):
+        place = met_by(distance, b_place, mesh_sizes)
+        slot = jnp.where(place == early, 2 * early + side, side * early + place)
+        panels[:, pl.ds(pl.multiple_of(slot * width, width), width)] = block
+
+    for array_ref, distances in zip(own_refs, own_distances, strict=True):
         for i, distance in enumerate(distances):
-            shift = (me_col ^ distance) - me_col
-            stored = lax.rem(shift + ratio * me_row + ratio - 1 + 2 * col_count, col_count)
-            place = b_place((stored // ratio) ^ me_row)
-            columns = pl.ds(pl.multiple_of(place * width, width), width)
-            panels_ref[:, columns] = array_ref[:, i * width : (i + 1) * width]
-
-
-def early_kernel(distances, b_place, mesh_sizes, row_ids_ref, c_keep_ref, *refs):
-    a_refs, refs = refs[: len(distances)], refs[len(distances) :]
-    early = mesh_sizes[0] - 1
-    b_refs, (total_ref, a_last_ref, keep_ref, panels) = refs[:early], refs[early:]
-    width = a_last_ref.shape[1]
-    put_in_order(b_place, mesh_sizes, width, zip(a_refs, distances, strict=True), panels)
-    a_last_ref[...] = panels[:, early * width :]
-    second = jnp.concatenate([b_ref[width:, :] for b_ref in b_refs], axis=0)
+            put(array_ref[:, i * width : (i + 1) * width], distance, 0)
+    panels[:, early * width : 2 * early * width] = jnp.zeros(
+        (panels.shape[0], early * width), panels.dtype
+    )
+    panels[:, (2 * early + 1) * width :] = jnp.zeros((panels.shape[0], width), panels.dtype)
+    for i, distance in enumerate(partner_distances):
+        put(partner_ref[:, i * width : (i + 1) * width], distance, 1)
+    tail_ref[...] = panels[:, 2 * early * width :]
+    for place, b_ref in enumerate(b_refs):
+        firsts_ref[place * width : (place + 1) * width, :] = b_ref[:width, :]
+    blocks = jnp.concatenate(
+        [b_ref[width:, :] for b_ref in b_refs] + [b_ref[:width, :] for b_ref in b_refs], axis=0
+    )
     for start in range(0, total_ref.shape[0], 2 * TILE):
         rows = pl.ds(start, 2 * TILE)
         total_ref[rows, :] = jnp.dot(
-            panels[rows, : early * width], second, preferred_element_type=jnp.float32
+            panels[rows, : 2 * early * width], blocks, preferred_element_type=jnp.float32
         )
     ids = row_ids_ref[...]
     which = lax.broadcasted_iota(jnp.int32, (ids.shape[0], c_keep_ref.shape[1]), 1)
@@ -96,42 +112,48 @@
     )
 
 
-def early_product(row_ids, c_keep, a_groups, b_blocks, b_place, mesh_sizes):
-    arrays, distances = zip(*a_groups, strict=True)
+def early_product(row_ids, c_keep, owns, partner, b_blocks, b_place, mesh_sizes):
+    arrays, distances = zip(*owns, strict=True)
+    partner_array, partner_distances = partner
     a_rows = arrays[0].shape[0]
     depth, columns = b_blocks[0].shape
-    width = depth // 2
-    return pl.pallas_call(
-        functools.partial(early_kernel, distances, b_place, mesh_sizes),
+    width, early = depth // 2, len(b_blocks)
+    return pl.pallas_call(
+        functools.partial(early_kernel, distances, partner_distances, b_place, mesh_sizes),
         out_shape=(
             pltpu.VMEM((a_rows, columns), jnp.float32),
-            pltpu.VMEM((a_rows, width), jnp.bfloat16),
+            pltpu.VMEM((a_rows, depth), jnp.bfloat16),
             pltpu.VMEM((row_ids.shape[0], columns), jnp.float32),
+            pltpu.VMEM(((early + 1) * width, columns), jnp.bfloat16),
         ),
-        in_specs=[VMEM] * (2 + len(arrays) + len(b_blocks)),
-        out_specs=(VMEM, VMEM, VMEM),
-        scratch_shapes=[pltpu.VMEM((a_rows, width * mesh_sizes[0]), jnp.bfloat16)],
+        in_specs=[VMEM] * (3 + len(arrays) + len(b_blocks)),
+        out_specs=(VMEM,) * 4,
+        scratch_shapes=[pltpu.VMEM((a_rows, (2 * early + 2) * width), jnp.bfloat16)],
         compiler_params=LIMITS,
-        cost_estimate=cost(2 * a_rows * width * len(b_blocks) * columns, 4 * a_rows * columns),
-    )(near(row_ids[:, None]), near(c_keep.T), *(near(block) for block in (*arrays, *b_blocks)))
-
-
-def last_kernel(distances, b_place, mesh_sizes, keep_ref, total_ref, a_last_ref, *refs):
-    row_count = mesh_sizes[0]
-    a_refs, refs = refs[: len(distances)], refs[len(distances) :]
-    b_refs, (out_ref, panels, out_tiles, out_sem) = refs[:row_count], refs[row_count:]
-    width = a_last_ref.shape[1]
-    put_in_order(b_place, mesh_sizes, width, zip(a_refs, distances, strict=True), panels)
-    panels[:, row_count * width :] = a_last_ref[...]
-    blocks = jnp.concatenate(
-        [b_ref[:width, :] for b_ref in b_refs] + [b_refs[-1][width:, :]], axis=0
-    )
+        cost_estimate=cost(2 * a_rows * width * early * columns, 4 * a_rows * columns),
+    )(
+        near(row_ids[:, None]),
+        near(c_keep.T),
+        *(near(block) for block in (*arrays, partner_array, *b_blocks)),
+    )
+
+
+def last_kernel(distances, b_place, mesh_sizes, keep_ref, total_ref, tail_ref, a_ref, b_ref, firsts_in_ref, out_ref, firsts_ref, out_tiles, out_sem):
+    width = b_ref.shape[0] // 2
+    firsts_ref[(mesh_sizes[0] - 1) * width :, :] = b_ref[:width, :]
+    panels = []
+    for distance in distances:
+        place = met_by(distance, b_place, mesh_sizes)
+        panels.append(firsts_ref[pl.ds(pl.multiple_of(place * width, width), width), :])
+    blocks = jnp.concatenate(panels + [b_ref[width:, :], b_ref[:width, :]], axis=0)
     rows = out_tiles.shape[1]
     writes = []
     for step in range(out_tiles.shape[0]):
         own = pl.ds(step * rows, rows)
         total = total_ref[own, :] + jnp.dot(
-            panels[own, :], blocks, preferred_element_type=jnp.float32
+            jnp.concatenate([a_ref[own, :], tail_ref[own, :]], axis=1),
+            blocks,
+            preferred_element_type=jnp.float32,
         )
         for i in range(rows // TILE):
             slot = step * rows // TILE + i
@@ -146,25 +168,28 @@
         write.wait()
 
 
-def last_product(keep, total, a_last, a_groups, b_blocks, b_place, mesh_sizes):
-    arrays, distances = zip(*a_groups, strict=True)
+def last_product(keep, total, tail, firsts, partner, b_last, b_place, mesh_sizes):
+    array, distances = partner
     a_rows, columns = total.shape
-    inner = a_last.shape[1] * (mesh_sizes[0] + 1)
+    inner = array.shape[1] + tail.shape[1]
     rows = 2 * TILE
     steps = a_rows // rows
     return pl.pallas_call(
         functools.partial(last_kernel, distances, b_place, mesh_sizes),
-        out_shape=jax.ShapeDtypeStruct((a_rows, columns), jnp.bfloat16),
-        in_specs=[VMEM] * (3 + len(arrays) + len(b_blocks)),
-        out_specs=ANY,
+        out_shape=(
+            jax.ShapeDtypeStruct((a_rows, columns), jnp.bfloat16),
+            pltpu.VMEM(firsts.shape, firsts.dtype),
+        ),
+        in_specs=[VMEM] * 6,
+        out_specs=(ANY, VMEM),
+        input_output_aliases={5: 1},
         scratch_shapes=[
-            pltpu.VMEM((a_rows, inner), jnp.bfloat16),
             pltpu.VMEM((steps, rows, columns), jnp.bfloat16),
             pltpu.SemaphoreType.DMA((steps,)),
         ],
         compiler_params=LIMITS,
         cost_estimate=cost(2 * a_rows * inner * columns, 6 * total.size),
-    )(*(near(array) for array in (keep, total, a_last, *arrays, *b_blocks)))
+    )(*(near(operand) for operand in (keep, total, tail, array, b_last, firsts)))[0]
 
 
 def swapped(block, axis, distance):
@@ -245,8 +270,10 @@
     a_eff, b_eff = masked(a_tiles, a_mask, b_tiles, b_mask)
     b_blocks, b_place = gathered_b(b_eff)
     owns, partners = gathered_a(a_eff)
-    total, a_last, keep = early_product(row_ids, c_keep, owns, b_blocks[:-1], b_place, sizes)
-    return last_product(keep, total, a_last, partners, b_blocks, b_place, sizes)
+    total, tail, keep, firsts = early_product(
+        row_ids, c_keep, owns, partners[0], b_blocks[:-1], b_place, sizes
+    )
+    return last_product(keep, total, tail, firsts, partners[1], b_blocks[-1], b_place, sizes)
 
 
 def solution(mesh):

time: 21.9 us -> 21.7 us (level)
  waiting for transfers between devices: 5.56 us -> 5.12 us
    pallas_call x1, Pallas kernels: 0.79 us -> 1.23 us  [early_product(): pl.pallas_call(functools.partial(early_kernel, distances, partner_distanc...]
    ppermute x5, waiting for transfers between devices: 4.86 us -> 4.51 us  [swapped(): lax.ppermute(block, axis, [(i, i ^ distance) for i in range(lax.axis_size...]
    pallas_call x1, Pallas kernels: 1.64 us -> 1.36 us  [last_product(): pl.pallas_call(functools.partial(last_kernel, distances, b_place, mesh_si...]
  transfers between devices with their start and end apart: 8 -> 8, of which waited for: 5 -> 5; matrix products, arithmetic and copies ran while one was open for 0% -> 0% of each run, Pallas kernels for 4% -> 6%
where the time goes in v4:
time: 21.7 us; the launch traced here: 21.5 us
  starting transfers between devices  12.4 us (57%)
  waiting for transfers between devices  5.12 us (24%)
  Pallas kernels  3.9 us (18%)
    ppermute x3, starting transfers between devices, crossed(): return lax.ppermute(block, ('row', 'col'), pairs)  8.04 us
    ppermute x5, waiting for transfers between devices, swapped(): lax.ppermute(block, axis, [(i, i ^ distance) for i in range(lax.axis_size...  4.51 us
    ppermute x5, starting transfers between devices, swapped(): lax.ppermute(block, axis, [(i, i ^ distance) for i in range(lax.axis_size...  4.31 us
    pallas_call x1, Pallas kernels, last_product(): pl.pallas_call(functools.partial(last_kernel, distances, b_place, mesh_si...  1.36 us
    pallas_call x1, Pallas kernels, early_product(): pl.pallas_call(functools.partial(early_kernel, distances, partner_distanc...  1.23 us
    pallas_call x1, Pallas kernels, masked(): pl.pallas_call(mask_kernel, out_shape=(pltpu.VMEM(a_tiles.shape, a_tiles....  1.22 us
    ppermute x3, waiting for transfers between devices, crossed(): return lax.ppermute(block, ('row', 'col'), pairs)  0.61 us
  transfers between devices with their start and end apart: 8, of which 5 were waited for; matrix products, arithmetic and copies ran while one was open for 0% of the time, Pallas kernels for 6%

profile of v4, /device:TPU:0, one launch (start us, length us, event | category | flops | bytes accessed | tf_op | source)
XLA Modules:
  0.0 21.5 jit_solution(5610269080820051057)
XLA Ops:
  0.0 0.0 copy-start.1
  0.0 0.0 copy-start
  0.0 1.2 %shard_map.64 = (bf16[512,128]{1,0:T(8,128)(2,1)S(1)}, bf16[256,768]{1,0:T(8,128)(2,1)S(1)}) custom-call(s32[2,8]{1,0:T(2,128)} %bitcast.4, s32[4,12]{1,0:T(4,128)} %b_mask_ref.1, bf16[512,128]{1,0:T(8,128)(2,1)} %a_ref.1, bf16[256,768]{1,0:T(8,128)(2,1)} %b_ref.1), custom_call_target="tpu_custom_call" | custom-call | flops 262144 | bytes 1048576 | tf_op jit(solution)/shard_map/pallas_call | solution.py:42
  1.2 3.0 %collective-permute-start.4 = (bf16[256,768]{1,0:T(8,128)(2,1)S(1)}, bf16[256,768]{1,0:T(8,128)(2,1)S(1)}, u32[]{:S(2)}, u32[]{:S(2)}) collective-permute-start(bf16[256,768]{1,0:T(8,128)(2,1)S(1)} %get-tuple-element.13.refs_3_), channel_id=1, source_target_pairs={{0,8},{1,17},{2,10},{3,19},{4,12},{5,21},{6,14},{7,23},{8,0},{9,25... | collective-permute-start | bytes 1179656 | tf_op jit(solution)/shard_map/ppermute | solution.py:206
  4.2 2.6 %collective-permute-start = (bf16[512,128]{1,0:T(8,128)(2,1)S(1)}, bf16[512,128]{1,0:T(8,128)(2,1)S(1)}, u32[]{:S(2)}, u32[]{:S(2)}) collective-permute-start(bf16[512,128]{1,0:T(8,128)(2,1)S(1)} %get-tuple-element.12.refs_0_), channel_id=1, source_target_pairs={{0,4},{1,5},{2,6},{3,7},{4,0},{5,1},{6,2},{7,3},{8,12},{9,13},{10,... | collective-permute-start | bytes 393224 | tf_op jit(solution)/shard_map/ppermute | solution.py:196
  6.8 1.3 %collective-permute-start.2 = (bf16[512,128]{1,0:T(8,128)(2,1)S(1)}, bf16[512,128]{1,0:T(8,128)(2,1)S(1)}, u32[]{:S(2)}, u32[]{:S(2)}) collective-permute-start(bf16[512,128]{1,0:T(8,128)(2,1)S(1)} %get-tuple-element.12.refs_0_), channel_id=1, source_target_pairs={{0,6},{1,7},{2,4},{3,5},{4,2},{5,3},{6,0},{7,1},{8,14},{9,15},{10,... | collective-permute-start | bytes 393224 | tf_op jit(solution)/shard_map/ppermute | solution.py:196
  8.2 1.5 %collective-permute-start.5 = (bf16[256,768]{1,0:T(8,128)(2,1)S(1)}, bf16[256,768]{1,0:T(8,128)(2,1)S(1)}, u32[]{:S(2)}, u32[]{:S(2)}) collective-permute-start(bf16[256,768]{1,0:T(8,128)(2,1)S(1)} %get-tuple-element.13.refs_3_), channel_id=1, source_target_pairs={{0,16},{1,9},{2,18},{3,11},{4,20},{5,13},{6,22},{7,15},{8,24},{9,1... | collective-permute-start | bytes 1179656 | tf_op jit(solution)/shard_map/ppermute | solution.py:206
  9.7 0.2 %collective-permute-start.1 = (bf16[512,128]{1,0:T(8,128)(2,1)S(1)}, bf16[512,128]{1,0:T(8,128)(2,1)S(1)}, u32[]{:S(2)}, u32[]{:S(2)}) collective-permute-start(bf16[512,128]{1,0:T(8,128)(2,1)S(1)} %get-tuple-element.12.refs_0_), channel_id=1, source_target_pairs={{0,2},{1,3},{2,0},{3,1},{4,6},{5,7},{6,4},{7,5},{8,10},{9,11},{10,... | collective-permute-start | bytes 393224 | tf_op jit(solution)/shard_map/ppermute | solution.py:196
  9.9 0.3 %collective-permute-done.4.refs_4_ = bf16[256,768]{1,0:T(8,128)(2,1)S(1)} collective-permute-done((bf16[256,768]{1,0:T(8,128)(2,1)S(1)}, bf16[256,768]{1,0:T(8,128)(2,1)S(1)}, u32[]{:S(2)}, u32[]{:S(2)}) %collective-permute-start.4) | collective-permute-done | bytes 393248 | tf_op jit(solution)/shard_map/ppermute | solution.py:206
  10.2 3.5 %collective-permute-start.7 = (bf16[256,768]{1,0:T(8,128)(2,1)S(1)}, bf16[256,768]{1,0:T(8,128)(2,1)S(1)}, u32[]{:S(2)}, u32[]{:S(2)}) collective-permute-start(bf16[256,768]{1,0:T(8,128)(2,1)S(1)} %collective-permute-done.4.refs_4_), channel_id=1, source_target_pairs={{0,16},{1,9},{2,18},{3,11},{4,20},{5,13},{6,22},{7,15},{8,24},{9,1... | collective-permute-start | bytes 1179656 | tf_op jit(solution)/shard_map/ppermute | solution.py:206
  13.7 3.2 %collective-permute-done.refs_1_ = bf16[512,128]{1,0:T(8,128)(2,1)S(1)} collective-permute-done((bf16[512,128]{1,0:T(8,128)(2,1)S(1)}, bf16[512,128]{1,0:T(8,128)(2,1)S(1)}, u32[]{:S(2)}, u32[]{:S(2)}) %collective-permute-start) | collective-permute-done | bytes 131104 | tf_op jit(solution)/shard_map/ppermute | solution.py:196
  17.0 0.1 collective-permute-start.3
  17.1 0.0 collective-permute-done.2.block_ref
  17.1 1.0 %collective-permute-done.1.refs_0_ = bf16[512,128]{1,0:T(8,128)(2,1)S(1)} collective-permute-done((bf16[512,128]{1,0:T(8,128)(2,1)S(1)}, bf16[512,128]{1,0:T(8,128)(2,1)S(1)}, u32[]{:S(2)}, u32[]{:S(2)}) %collective-permute-start.1) | collective-permute-done | bytes 131104 | tf_op jit(solution)/shard_map/ppermute | solution.py:196
  18.1 0.1 collective-permute-start.6
  18.2 0.0 copy-done.1
  18.2 0.1 copy.9.row_ids_ref
  18.3 0.3 %collective-permute-done.3.refs_2_ = bf16[512,256]{1,0:T(8,128)(2,1)S(1)} collective-permute-done((bf16[512,256]{1,0:T(8,128)(2,1)S(1)}, bf16[512,256]{1,0:T(8,128)(2,1)S(1)}, u32[]{:S(2)}, u32[]{:S(2)}) %collective-permute-start.3) | collective-permute-done | bytes 262176 | tf_op jit(solution)/shard_map/ppermute | solution.py:196
  18.6 0.0 collective-permute-done.5.refs_5_
  18.6 0.0 copy-done
  18.6 1.2 %shard_map.68 = (f32[512,768]{1,0:T(8,128)S(1)}, bf16[512,256]{1,0:T(8,128)(2,1)S(1)}, f32[8,768]{1,0:T(8,128)S(1)}, bf16[512,768]{1,0:T(8,128)(2,1)S(1)}) custom-call(s32[8,1]{1,0:T(8,128)S(1)} %copy.9.row_ids_ref, s32[12,32]{1,0:T(8,128)S(1)} %bitcast.3, bf16[512,256]{1,0:T(8,128)(2,1)S(1)} %shard_map.65.refs_0_, bf16[512,256]{1,0:T(8,128)(2,1)S(1)} %shard_map.67.refs_1_, ...), custom_call_target="tpu_custom_call" | custom-call | flops 301989888 | bytes 1572864 | tf_op jit(solution)/shard_map/pallas_call | solution.py:121
  19.8 0.0 collective-permute-done.6.a_ref
  19.8 0.3 %collective-permute-done.7.b_ref = bf16[256,768]{1,0:T(8,128)(2,1)S(1)} collective-permute-done((bf16[256,768]{1,0:T(8,128)(2,1)S(1)}, bf16[256,768]{1,0:T(8,128)(2,1)S(1)}, u32[]{:S(2)}, u32[]{:S(2)}) %collective-permute-start.7) | collective-permute-done | bytes 393248 | tf_op jit(solution)/shard_map/ppermute | solution.py:206
  20.2 1.4 %shard_map.69 = (bf16[512,768]{1,0:T(8,128)(2,1)}, bf16[512,768]{1,0:T(8,128)(2,1)S(1)}) custom-call(f32[8,768]{1,0:T(8,128)S(1)} %get-tuple-element.14.keep_ref, f32[512,768]{1,0:T(8,128)S(1)} %get-tuple-element.15.total_ref, bf16[512,256]{1,0:T(8,128)(2,1)S(1)} %get-tuple-element.16.tail_ref, ...), custom_call_target="tpu_custom_call", output_to_operand_aliasing={{1}: (5, {})} | custom-call | flops 402653184 | bytes 2359296 | tf_op jit(solution)/shard_map/pallas_call | solution.py:177
  (3 shorter events, 0.1 us)
Async XLA Ops:
  0.0 18.2 %copy-start.1 = (s32[8]{0:T(128)S(1)}, s32[8]{0:T(128)}, u32[]{:S(2)}) copy-start(s32[8]{0:T(128)} %param.6) | copy-start | bytes 100
  0.0 18.6 %copy-start = (s32[32,12]{0,1:T(8,128)S(1)}, s32[32,12]{0,1:T(8,128)}, u32[]{:S(2)}) copy-start(s32[32,12]{0,1:T(8,128)} %param.11) | copy-start | bytes 4612
  1.2 9.0 %collective-permute-start.4 = (bf16[256,768]{1,0:T(8,128)(2,1)S(1)}, bf16[256,768]{1,0:T(8,128)(2,1)S(1)}, u32[]{:S(2)}, u32[]{:S(2)}) collective-permute-start(bf16[256,768]{1,0:T(8,128)(2,1)S(1)} %get-tuple-element.13.refs_3_), channel_id=1, source_target_pairs={{0,8},{1,17},{2,10},{3,19},{4,12},{5,21},{6,14},{7,23},{8,0},{9,25... | collective-permute-start | bytes 1179656 | tf_op jit(solution)/shard_map/ppermute | solution.py:206
  4.2 12.7 %collective-permute-start = (bf16[512,128]{1,0:T(8,128)(2,1)S(1)}, bf16[512,128]{1,0:T(8,128)(2,1)S(1)}, u32[]{:S(2)}, u32[]{:S(2)}) collective-permute-start(bf16[512,128]{1,0:T(8,128)(2,1)S(1)} %get-tuple-element.12.refs_0_), channel_id=1, source_target_pairs={{0,4},{1,5},{2,6},{3,7},{4,0},{5,1},{6,2},{7,3},{8,12},{9,13},{10,... | collective-permute-start | bytes 393224 | tf_op jit(solution)/shard_map/ppermute | solution.py:196
  6.8 10.2 %collective-permute-start.2 = (bf16[512,128]{1,0:T(8,128)(2,1)S(1)}, bf16[512,128]{1,0:T(8,128)(2,1)S(1)}, u32[]{:S(2)}, u32[]{:S(2)}) collective-permute-start(bf16[512,128]{1,0:T(8,128)(2,1)S(1)} %get-tuple-element.12.refs_0_), channel_id=1, source_target_pairs={{0,6},{1,7},{2,4},{3,5},{4,2},{5,3},{6,0},{7,1},{8,14},{9,15},{10,... | collective-permute-start | bytes 393224 | tf_op jit(solution)/shard_map/ppermute | solution.py:196
  8.2 10.4 %collective-permute-start.5 = (bf16[256,768]{1,0:T(8,128)(2,1)S(1)}, bf16[256,768]{1,0:T(8,128)(2,1)S(1)}, u32[]{:S(2)}, u32[]{:S(2)}) collective-permute-start(bf16[256,768]{1,0:T(8,128)(2,1)S(1)} %get-tuple-element.13.refs_3_), channel_id=1, source_target_pairs={{0,16},{1,9},{2,18},{3,11},{4,20},{5,13},{6,22},{7,15},{8,24},{9,1... | collective-permute-start | bytes 1179656 | tf_op jit(solution)/shard_map/ppermute | solution.py:206
  9.7 8.4 %collective-permute-start.1 = (bf16[512,128]{1,0:T(8,128)(2,1)S(1)}, bf16[512,128]{1,0:T(8,128)(2,1)S(1)}, u32[]{:S(2)}, u32[]{:S(2)}) collective-permute-start(bf16[512,128]{1,0:T(8,128)(2,1)S(1)} %get-tuple-element.12.refs_0_), channel_id=1, source_target_pairs={{0,2},{1,3},{2,0},{3,1},{4,6},{5,7},{6,4},{7,5},{8,10},{9,11},{10,... | collective-permute-start | bytes 393224 | tf_op jit(solution)/shard_map/ppermute | solution.py:196
  10.2 10.0 %collective-permute-start.7 = (bf16[256,768]{1,0:T(8,128)(2,1)S(1)}, bf16[256,768]{1,0:T(8,128)(2,1)S(1)}, u32[]{:S(2)}, u32[]{:S(2)}) collective-permute-start(bf16[256,768]{1,0:T(8,128)(2,1)S(1)} %collective-permute-done.4.refs_4_), channel_id=1, source_target_pairs={{0,16},{1,9},{2,18},{3,11},{4,20},{5,13},{6,22},{7,15},{8,24},{9,1... | collective-permute-start | bytes 1179656 | tf_op jit(solution)/shard_map/ppermute | solution.py:206
  17.0 1.6 %collective-permute-start.3 = (bf16[512,256]{1,0:T(8,128)(2,1)S(1)}, bf16[512,256]{1,0:T(8,128)(2,1)S(1)}, u32[]{:S(2)}, u32[]{:S(2)}) collective-permute-start(bf16[512,256]{1,0:T(8,128)(2,1)S(1)} %shard_map.65.refs_0_), channel_id=1, source_target_pairs={{0,1},{1,0},{2,3},{3,2},{4,5},{5,4},{6,7},{7,6},{8,9},{9,8},{10,11... | collective-permute-start | bytes 786440 | tf_op jit(solution)/shard_map/ppermute | solution.py:196
  18.1 1.7 %collective-permute-start.6 = (bf16[512,256]{1,0:T(8,128)(2,1)S(1)}, bf16[512,256]{1,0:T(8,128)(2,1)S(1)}, u32[]{:S(2)}, u32[]{:S(2)}) collective-permute-start(bf16[512,256]{1,0:T(8,128)(2,1)S(1)} %shard_map.67.refs_1_), channel_id=1, source_target_pairs={{0,1},{1,0},{2,3},{3,2},{4,5},{5,4},{6,7},{7,6},{8,9},{9,8},{10,11... | collective-permute-start | bytes 786440 | tf_op jit(solution)/shard_map/ppermute | solution.py:196

commit v5 on v4

--- a/solution.py
+++ b/solution.py
@@ -77,16 +77,15 @@
 
     def put(block, distance, side):
         place = met_by(distance, b_place, mesh_sizes)
-        slot = jnp.where(place == early, 2 * early + side, side * early + place)
+        slot = jnp.where(place == early, 2 * early + 1 - side, side * early + place)
         panels[:, pl.ds(pl.multiple_of(slot * width, width), width)] = block
 
     for array_ref, distances in zip(own_refs, own_distances, strict=True):
         for i, distance in enumerate(distances):
             put(array_ref[:, i * width : (i + 1) * width], distance, 0)
-    panels[:, early * width : 2 * early * width] = jnp.zeros(
-        (panels.shape[0], early * width), panels.dtype
-    )
-    panels[:, (2 * early + 1) * width :] = jnp.zeros((panels.shape[0], width), panels.dtype)
+    panels[:, early * width : (2 * early + 1) * width] = jnp.zeros(
+        (panels.shape[0], (early + 1) * width), panels.dtype
+    )
     for i, distance in enumerate(partner_distances):
         put(partner_ref[:, i * width : (i + 1) * width], distance, 1)
     tail_ref[...] = panels[:, 2 * early * width :]
@@ -101,12 +100,12 @@
             panels[rows, : 2 * early * width], blocks, preferred_element_type=jnp.float32
         )
     ids = row_ids_ref[...]
-    which = lax.broadcasted_iota(jnp.int32, (ids.shape[0], c_keep_ref.shape[1]), 1)
+    which = lax.broadcasted_iota(jnp.int32, (c_keep_ref.shape[1], ids.shape[1]), 0)
     keep_ref[...] = spread(
         lax.dot_general(
             (ids == which).astype(jnp.float32),
             c_keep_ref[...].astype(jnp.float32),
-            (((1,), (1,)), ((), ())),
+            (((0,), (1,)), ((), ())),
             preferred_element_type=jnp.float32,
         )
     )
@@ -132,7 +131,7 @@
         compiler_params=LIMITS,
         cost_estimate=cost(2 * a_rows * width * early * columns, 4 * a_rows * columns),
     )(
-        near(row_ids[:, None]),
+        near(row_ids[None, :]),
         near(c_keep.T),
         *(near(block) for block in (*arrays, partner_array, *b_blocks)),
     )
@@ -145,16 +144,15 @@
     for distance in distances:
         place = met_by(distance, b_place, mesh_sizes)
         panels.append(firsts_ref[pl.ds(pl.multiple_of(place * width, width), width), :])
-    blocks = jnp.concatenate(panels + [b_ref[width:, :], b_ref[:width, :]], axis=0)
+    blocks = jnp.concatenate(panels, axis=0)
     rows = out_tiles.shape[1]
     writes = []
     for step in range(out_tiles.shape[0]):
         own = pl.ds(step * rows, rows)
         total = total_ref[own, :] + jnp.dot(
-            jnp.concatenate([a_ref[own, :], tail_ref[own, :]], axis=1),
-            blocks,
-            preferred_element_type=jnp.float32,
-        )
+            tail_ref[own, :], b_ref[...], preferred_element_type=jnp.float32
+        )
+        total = total + jnp.dot(a_ref[own, :], blocks, preferred_element_type=jnp.float32)
         for i in range(rows // TILE):
             slot = step * rows // TILE + i
             out_tiles[step, pl.ds(i * TILE, TILE), :] = (

time: 21.7 us -> 21.6 us (level)
  no operation moved by 1% of the time
where the time goes in v5:
time: 21.6 us; the launch traced here: 21.5 us
  starting transfers between devices  12.4 us (57%)
  waiting for transfers between devices  5.23 us (24%)
  Pallas kernels  3.85 us (18%)
    ppermute x3, starting transfers between devices, crossed(): return lax.ppermute(block, ('row', 'col'), pairs)  8.04 us
    ppermute x5, waiting for transfers between devices, swapped(): lax.ppermute(block, axis, [(i, i ^ distance) for i in range(lax.axis_size...  4.6 us
    ppermute x5, starting transfers between devices, swapped(): lax.ppermute(block, axis, [(i, i ^ distance) for i in range(lax.axis_size...  4.31 us
    pallas_call x1, Pallas kernels, last_product(): pl.pallas_call(functools.partial(last_kernel, distances, b_place, mesh_si...  1.33 us
    pallas_call x1, Pallas kernels, masked(): pl.pallas_call(mask_kernel, out_shape=(pltpu.VMEM(a_tiles.shape, a_tiles....  1.22 us
    pallas_call x1, Pallas kernels, early_product(): pl.pallas_call(functools.partial(early_kernel, distances, partner_distanc...  1.2 us
    ppermute x3, waiting for transfers between devices, crossed(): return lax.ppermute(block, ('row', 'col'), pairs)  0.63 us
  transfers between devices with their start and end apart: 8, of which 5 were waited for; matrix products, arithmetic and copies ran while one was open for 0% of the time, Pallas kernels for 6%

profile of v5, /device:TPU:0, one launch (start us, length us, event | category | flops | bytes accessed | tf_op | source)
XLA Modules:
  0.0 21.5 jit_solution(13446869451266822627)
XLA Ops:
  0.0 0.0 copy-start
  0.0 0.0 copy-start.1
  0.0 1.2 %shard_map.64 = (bf16[512,128]{1,0:T(8,128)(2,1)S(1)}, bf16[256,768]{1,0:T(8,128)(2,1)S(1)}) custom-call(s32[2,8]{1,0:T(2,128)} %bitcast.5, s32[4,12]{1,0:T(4,128)} %b_mask_ref.1, bf16[512,128]{1,0:T(8,128)(2,1)} %a_ref.1, bf16[256,768]{1,0:T(8,128)(2,1)} %b_ref.1), custom_call_target="tpu_custom_call" | custom-call | flops 262144 | bytes 1048576 | tf_op jit(solution)/shard_map/pallas_call | solution.py:42
  1.2 3.0 %collective-permute-start.4 = (bf16[256,768]{1,0:T(8,128)(2,1)S(1)}, bf16[256,768]{1,0:T(8,128)(2,1)S(1)}, u32[]{:S(2)}, u32[]{:S(2)}) collective-permute-start(bf16[256,768]{1,0:T(8,128)(2,1)S(1)} %get-tuple-element.13.refs_3_), channel_id=1, source_target_pairs={{0,8},{1,17},{2,10},{3,19},{4,12},{5,21},{6,14},{7,23},{8,0},{9,25... | collective-permute-start | bytes 1179656 | tf_op jit(solution)/shard_map/ppermute | solution.py:204
  4.2 2.6 %collective-permute-start = (bf16[512,128]{1,0:T(8,128)(2,1)S(1)}, bf16[512,128]{1,0:T(8,128)(2,1)S(1)}, u32[]{:S(2)}, u32[]{:S(2)}) collective-permute-start(bf16[512,128]{1,0:T(8,128)(2,1)S(1)} %get-tuple-element.12.refs_0_), channel_id=1, source_target_pairs={{0,4},{1,5},{2,6},{3,7},{4,0},{5,1},{6,2},{7,3},{8,12},{9,13},{10,... | collective-permute-start | bytes 393224 | tf_op jit(solution)/shard_map/ppermute | solution.py:194
  6.8 1.3 %collective-permute-start.2 = (bf16[512,128]{1,0:T(8,128)(2,1)S(1)}, bf16[512,128]{1,0:T(8,128)(2,1)S(1)}, u32[]{:S(2)}, u32[]{:S(2)}) collective-permute-start(bf16[512,128]{1,0:T(8,128)(2,1)S(1)} %get-tuple-element.12.refs_0_), channel_id=1, source_target_pairs={{0,6},{1,7},{2,4},{3,5},{4,2},{5,3},{6,0},{7,1},{8,14},{9,15},{10,... | collective-permute-start | bytes 393224 | tf_op jit(solution)/shard_map/ppermute | solution.py:194
  8.2 1.5 %collective-permute-start.5 = (bf16[256,768]{1,0:T(8,128)(2,1)S(1)}, bf16[256,768]{1,0:T(8,128)(2,1)S(1)}, u32[]{:S(2)}, u32[]{:S(2)}) collective-permute-start(bf16[256,768]{1,0:T(8,128)(2,1)S(1)} %get-tuple-element.13.refs_3_), channel_id=1, source_target_pairs={{0,16},{1,9},{2,18},{3,11},{4,20},{5,13},{6,22},{7,15},{8,24},{9,1... | collective-permute-start | bytes 1179656 | tf_op jit(solution)/shard_map/ppermute | solution.py:204
  9.7 0.2 %collective-permute-start.1 = (bf16[512,128]{1,0:T(8,128)(2,1)S(1)}, bf16[512,128]{1,0:T(8,128)(2,1)S(1)}, u32[]{:S(2)}, u32[]{:S(2)}) collective-permute-start(bf16[512,128]{1,0:T(8,128)(2,1)S(1)} %get-tuple-element.12.refs_0_), channel_id=1, source_target_pairs={{0,2},{1,3},{2,0},{3,1},{4,6},{5,7},{6,4},{7,5},{8,10},{9,11},{10,... | collective-permute-start | bytes 393224 | tf_op jit(solution)/shard_map/ppermute | solution.py:194
  9.9 0.3 %collective-permute-done.4.refs_4_ = bf16[256,768]{1,0:T(8,128)(2,1)S(1)} collective-permute-done((bf16[256,768]{1,0:T(8,128)(2,1)S(1)}, bf16[256,768]{1,0:T(8,128)(2,1)S(1)}, u32[]{:S(2)}, u32[]{:S(2)}) %collective-permute-start.4) | collective-permute-done | bytes 393248 | tf_op jit(solution)/shard_map/ppermute | solution.py:204
  10.2 3.5 %collective-permute-start.7 = (bf16[256,768]{1,0:T(8,128)(2,1)S(1)}, bf16[256,768]{1,0:T(8,128)(2,1)S(1)}, u32[]{:S(2)}, u32[]{:S(2)}) collective-permute-start(bf16[256,768]{1,0:T(8,128)(2,1)S(1)} %collective-permute-done.4.refs_4_), channel_id=1, source_target_pairs={{0,16},{1,9},{2,18},{3,11},{4,20},{5,13},{6,22},{7,15},{8,24},{9,1... | collective-permute-start | bytes 1179656 | tf_op jit(solution)/shard_map/ppermute | solution.py:204
  13.7 3.2 %collective-permute-done.refs_1_ = bf16[512,128]{1,0:T(8,128)(2,1)S(1)} collective-permute-done((bf16[512,128]{1,0:T(8,128)(2,1)S(1)}, bf16[512,128]{1,0:T(8,128)(2,1)S(1)}, u32[]{:S(2)}, u32[]{:S(2)}) %collective-permute-start) | collective-permute-done | bytes 131104 | tf_op jit(solution)/shard_map/ppermute | solution.py:194
  17.0 0.1 collective-permute-start.3
  17.1 0.0 collective-permute-done.2.block_ref
  17.1 1.0 %collective-permute-done.1.refs_0_ = bf16[512,128]{1,0:T(8,128)(2,1)S(1)} collective-permute-done((bf16[512,128]{1,0:T(8,128)(2,1)S(1)}, bf16[512,128]{1,0:T(8,128)(2,1)S(1)}, u32[]{:S(2)}, u32[]{:S(2)}) %collective-permute-start.1) | collective-permute-done | bytes 131104 | tf_op jit(solution)/shard_map/ppermute | solution.py:194
  18.1 0.1 collective-permute-start.6
  18.2 0.4 %collective-permute-done.3.refs_2_ = bf16[512,256]{1,0:T(8,128)(2,1)S(1)} collective-permute-done((bf16[512,256]{1,0:T(8,128)(2,1)S(1)}, bf16[512,256]{1,0:T(8,128)(2,1)S(1)}, u32[]{:S(2)}, u32[]{:S(2)}) %collective-permute-start.3) | collective-permute-done | bytes 262176 | tf_op jit(solution)/shard_map/ppermute | solution.py:194
  18.6 0.0 collective-permute-done.5.refs_5_
  18.6 0.0 copy-done
  18.6 0.0 copy-done.1
  18.6 1.2 %shard_map.68 = (f32[512,768]{1,0:T(8,128)S(1)}, bf16[512,256]{1,0:T(8,128)(2,1)S(1)}, f32[8,768]{1,0:T(8,128)S(1)}, bf16[512,768]{1,0:T(8,128)(2,1)S(1)}) custom-call(s32[1,8]{1,0:T(1,128)S(1)} %bitcast.4, s32[12,32]{1,0:T(8,128)S(1)} %bitcast.3, bf16[512,256]{1,0:T(8,128)(2,1)S(1)} %shard_map.65.refs_0_, bf16[512,256]{1,0:T(8,128)(2,1)S(1)} %shard_map.67.refs_1_, ...), custom_call_target="tpu_custom_call" | custom-call | flops 301989888 | bytes 1572864 | tf_op jit(solution)/shard_map/pallas_call | solution.py:120
  19.8 0.0 collective-permute-done.6.a_ref
  19.8 0.4 %collective-permute-done.7.b_ref = bf16[256,768]{1,0:T(8,128)(2,1)S(1)} collective-permute-done((bf16[256,768]{1,0:T(8,128)(2,1)S(1)}, bf16[256,768]{1,0:T(8,128)(2,1)S(1)}, u32[]{:S(2)}, u32[]{:S(2)}) %collective-permute-start.7) | collective-permute-done | bytes 393248 | tf_op jit(solution)/shard_map/ppermute | solution.py:204
  20.2 1.3 %shard_map.69 = (bf16[512,768]{1,0:T(8,128)(2,1)}, bf16[512,768]{1,0:T(8,128)(2,1)S(1)}) custom-call(f32[8,768]{1,0:T(8,128)S(1)} %get-tuple-element.14.keep_ref, f32[512,768]{1,0:T(8,128)S(1)} %get-tuple-element.15.total_ref, bf16[512,256]{1,0:T(8,128)(2,1)S(1)} %get-tuple-element.16.tail_ref, ...), custom_call_target="tpu_custom_call", output_to_operand_aliasing={{1}: (5, {})} | custom-call | flops 402653184 | bytes 2359296 | tf_op jit(solution)/shard_map/pallas_call | solution.py:175
  (3 shorter events, 0.1 us)
Async XLA Ops:
  0.0 18.6 %copy-start = (s32[32,12]{0,1:T(8,128)S(1)}, s32[32,12]{0,1:T(8,128)}, u32[]{:S(2)}) copy-start(s32[32,12]{0,1:T(8,128)} %param.11) | copy-start | bytes 4612
  0.0 18.6 %copy-start.1 = (s32[8]{0:T(128)S(1)}, s32[8]{0:T(128)}, u32[]{:S(2)}) copy-start(s32[8]{0:T(128)} %param.6) | copy-start | bytes 100
  1.2 9.0 %collective-permute-start.4 = (bf16[256,768]{1,0:T(8,128)(2,1)S(1)}, bf16[256,768]{1,0:T(8,128)(2,1)S(1)}, u32[]{:S(2)}, u32[]{:S(2)}) collective-permute-start(bf16[256,768]{1,0:T(8,128)(2,1)S(1)} %get-tuple-element.13.refs_3_), channel_id=1, source_target_pairs={{0,8},{1,17},{2,10},{3,19},{4,12},{5,21},{6,14},{7,23},{8,0},{9,25... | collective-permute-start | bytes 1179656 | tf_op jit(solution)/shard_map/ppermute | solution.py:204
  4.2 12.7 %collective-permute-start = (bf16[512,128]{1,0:T(8,128)(2,1)S(1)}, bf16[512,128]{1,0:T(8,128)(2,1)S(1)}, u32[]{:S(2)}, u32[]{:S(2)}) collective-permute-start(bf16[512,128]{1,0:T(8,128)(2,1)S(1)} %get-tuple-element.12.refs_0_), channel_id=1, source_target_pairs={{0,4},{1,5},{2,6},{3,7},{4,0},{5,1},{6,2},{7,3},{8,12},{9,13},{10,... | collective-permute-start | bytes 393224 | tf_op jit(solution)/shard_map/ppermute | solution.py:194
  6.8 10.2 %collective-permute-start.2 = (bf16[512,128]{1,0:T(8,128)(2,1)S(1)}, bf16[512,128]{1,0:T(8,128)(2,1)S(1)}, u32[]{:S(2)}, u32[]{:S(2)}) collective-permute-start(bf16[512,128]{1,0:T(8,128)(2,1)S(1)} %get-tuple-element.12.refs_0_), channel_id=1, source_target_pairs={{0,6},{1,7},{2,4},{3,5},{4,2},{5,3},{6,0},{7,1},{8,14},{9,15},{10,... | collective-permute-start | bytes 393224 | tf_op jit(solution)/shard_map/ppermute | solution.py:194
  8.2 10.4 %collective-permute-start.5 = (bf16[256,768]{1,0:T(8,128)(2,1)S(1)}, bf16[256,768]{1,0:T(8,128)(2,1)S(1)}, u32[]{:S(2)}, u32[]{:S(2)}) collective-permute-start(bf16[256,768]{1,0:T(8,128)(2,1)S(1)} %get-tuple-element.13.refs_3_), channel_id=1, source_target_pairs={{0,16},{1,9},{2,18},{3,11},{4,20},{5,13},{6,22},{7,15},{8,24},{9,1... | collective-permute-start | bytes 1179656 | tf_op jit(solution)/shard_map/ppermute | solution.py:204
  9.7 8.4 %collective-permute-start.1 = (bf16[512,128]{1,0:T(8,128)(2,1)S(1)}, bf16[512,128]{1,0:T(8,128)(2,1)S(1)}, u32[]{:S(2)}, u32[]{:S(2)}) collective-permute-start(bf16[512,128]{1,0:T(8,128)(2,1)S(1)} %get-tuple-element.12.refs_0_), channel_id=1, source_target_pairs={{0,2},{1,3},{2,0},{3,1},{4,6},{5,7},{6,4},{7,5},{8,10},{9,11},{10,... | collective-permute-start | bytes 393224 | tf_op jit(solution)/shard_map/ppermute | solution.py:194
  10.2 10.0 %collective-permute-start.7 = (bf16[256,768]{1,0:T(8,128)(2,1)S(1)}, bf16[256,768]{1,0:T(8,128)(2,1)S(1)}, u32[]{:S(2)}, u32[]{:S(2)}) collective-permute-start(bf16[256,768]{1,0:T(8,128)(2,1)S(1)} %collective-permute-done.4.refs_4_), channel_id=1, source_target_pairs={{0,16},{1,9},{2,18},{3,11},{4,20},{5,13},{6,22},{7,15},{8,24},{9,1... | collective-permute-start | bytes 1179656 | tf_op jit(solution)/shard_map/ppermute | solution.py:204
  17.0 1.6 %collective-permute-start.3 = (bf16[512,256]{1,0:T(8,128)(2,1)S(1)}, bf16[512,256]{1,0:T(8,128)(2,1)S(1)}, u32[]{:S(2)}, u32[]{:S(2)}) collective-permute-start(bf16[512,256]{1,0:T(8,128)(2,1)S(1)} %shard_map.65.refs_0_), channel_id=1, source_target_pairs={{0,1},{1,0},{2,3},{3,2},{4,5},{5,4},{6,7},{7,6},{8,9},{9,8},{10,11... | collective-permute-start | bytes 786440 | tf_op jit(solution)/shard_map/ppermute | solution.py:194
  18.1 1.7 %collective-permute-start.6 = (bf16[512,256]{1,0:T(8,128)(2,1)S(1)}, bf16[512,256]{1,0:T(8,128)(2,1)S(1)}, u32[]{:S(2)}, u32[]{:S(2)}) collective-permute-start(bf16[512,256]{1,0:T(8,128)(2,1)S(1)} %shard_map.67.refs_1_), channel_id=1, source_target_pairs={{0,1},{1,0},{2,3},{3,2},{4,5},{5,4},{6,7},{7,6},{8,9},{9,8},{10,11... | collective-permute-start | bytes 786440 | tf_op jit(solution)/shard_map/ppermute | solution.py:194

commit v6 on v4

--- a/solution.py
+++ b/solution.py
@@ -160,10 +160,14 @@
             out_tiles[step, pl.ds(i * TILE, TILE), :] = (
                 total[i * TILE : (i + 1) * TILE] * keep_ref[slot : slot + 1, :]
             ).astype(jnp.bfloat16)
-        writes.append(
-            pltpu.make_async_copy(out_tiles.at[step], out_ref.at[own, :], out_sem.at[step])
-        )
-        writes[-1].start()
+            writes.append(
+                pltpu.make_async_copy(
+                    out_tiles.at[step, pl.ds(i * TILE, TILE)],
+                    out_ref.at[pl.ds(slot * TILE, TILE), :],
+                    out_sem.at[slot],
+                )
+            )
+            writes[-1].start()
     for write in writes:
         write.wait()
 
@@ -185,7 +189,7 @@
         input_output_aliases={5: 1},
         scratch_shapes=[
             pltpu.VMEM((steps, rows, columns), jnp.bfloat16),
-            pltpu.SemaphoreType.DMA((steps,)),
+            pltpu.SemaphoreType.DMA((a_rows // TILE,)),
         ],
         compiler_params=LIMITS,
         cost_estimate=cost(2 * a_rows * inner * columns, 6 * total.size),

time: 21.7 us -> 21.7 us (level)
  no operation moved by 1% of the time
where the time goes in v6:
time: 21.7 us; the launch traced here: 21.5 us
  starting transfers between devices  12.4 us (57%)
  waiting for transfers between devices  5.12 us (24%)
  Pallas kernels  3.93 us (18%)
    ppermute x3, starting transfers between devices, crossed(): return lax.ppermute(block, ('row', 'col'), pairs)  8.04 us
    ppermute x5, waiting for transfers between devices, swapped(): lax.ppermute(block, axis, [(i, i ^ distance) for i in range(lax.axis_size...  4.51 us
    ppermute x5, starting transfers between devices, swapped(): lax.ppermute(block, axis, [(i, i ^ distance) for i in range(lax.axis_size...  4.31 us
    pallas_call x1, Pallas kernels, last_product(): pl.pallas_call(functools.partial(last_kernel, distances, b_place, mesh_si...  1.38 us
    pallas_call x1, Pallas kernels, early_product(): pl.pallas_call(functools.partial(early_kernel, distances, partner_distanc...  1.23 us
    pallas_call x1, Pallas kernels, masked(): pl.pallas_call(mask_kernel, out_shape=(pltpu.VMEM(a_tiles.shape, a_tiles....  1.22 us
    ppermute x3, waiting for transfers between devices, crossed(): return lax.ppermute(block, ('row', 'col'), pairs)  0.61 us
  transfers between devices with their start and end apart: 8, of which 5 were waited for; matrix products, arithmetic and copies ran while one was open for 0% of the time, Pallas kernels for 6%

profile of v6, /device:TPU:0, one launch (start us, length us, event | category | flops | bytes accessed | tf_op | source)
XLA Modules:
  0.0 21.5 jit_solution(7738932312332063767)
XLA Ops:
  0.0 0.0 copy-start.1
  0.0 0.0 copy-start
  0.0 1.2 %shard_map.64 = (bf16[512,128]{1,0:T(8,128)(2,1)S(1)}, bf16[256,768]{1,0:T(8,128)(2,1)S(1)}) custom-call(s32[2,8]{1,0:T(2,128)} %bitcast.4, s32[4,12]{1,0:T(4,128)} %b_mask_ref.1, bf16[512,128]{1,0:T(8,128)(2,1)} %a_ref.1, bf16[256,768]{1,0:T(8,128)(2,1)} %b_ref.1), custom_call_target="tpu_custom_call" | custom-call | flops 262144 | bytes 1048576 | tf_op jit(solution)/shard_map/pallas_call | solution.py:42
  1.2 3.0 %collective-permute-start.4 = (bf16[256,768]{1,0:T(8,128)(2,1)S(1)}, bf16[256,768]{1,0:T(8,128)(2,1)S(1)}, u32[]{:S(2)}, u32[]{:S(2)}) collective-permute-start(bf16[256,768]{1,0:T(8,128)(2,1)S(1)} %get-tuple-element.13.refs_3_), channel_id=1, source_target_pairs={{0,8},{1,17},{2,10},{3,19},{4,12},{5,21},{6,14},{7,23},{8,0},{9,25... | collective-permute-start | bytes 1179656 | tf_op jit(solution)/shard_map/ppermute | solution.py:210
  4.2 2.6 %collective-permute-start = (bf16[512,128]{1,0:T(8,128)(2,1)S(1)}, bf16[512,128]{1,0:T(8,128)(2,1)S(1)}, u32[]{:S(2)}, u32[]{:S(2)}) collective-permute-start(bf16[512,128]{1,0:T(8,128)(2,1)S(1)} %get-tuple-element.12.refs_0_), channel_id=1, source_target_pairs={{0,4},{1,5},{2,6},{3,7},{4,0},{5,1},{6,2},{7,3},{8,12},{9,13},{10,... | collective-permute-start | bytes 393224 | tf_op jit(solution)/shard_map/ppermute | solution.py:200
  6.8 1.3 %collective-permute-start.2 = (bf16[512,128]{1,0:T(8,128)(2,1)S(1)}, bf16[512,128]{1,0:T(8,128)(2,1)S(1)}, u32[]{:S(2)}, u32[]{:S(2)}) collective-permute-start(bf16[512,128]{1,0:T(8,128)(2,1)S(1)} %get-tuple-element.12.refs_0_), channel_id=1, source_target_pairs={{0,6},{1,7},{2,4},{3,5},{4,2},{5,3},{6,0},{7,1},{8,14},{9,15},{10,... | collective-permute-start | bytes 393224 | tf_op jit(solution)/shard_map/ppermute | solution.py:200
  8.2 1.5 %collective-permute-start.5 = (bf16[256,768]{1,0:T(8,128)(2,1)S(1)}, bf16[256,768]{1,0:T(8,128)(2,1)S(1)}, u32[]{:S(2)}, u32[]{:S(2)}) collective-permute-start(bf16[256,768]{1,0:T(8,128)(2,1)S(1)} %get-tuple-element.13.refs_3_), channel_id=1, source_target_pairs={{0,16},{1,9},{2,18},{3,11},{4,20},{5,13},{6,22},{7,15},{8,24},{9,1... | collective-permute-start | bytes 1179656 | tf_op jit(solution)/shard_map/ppermute | solution.py:210
  9.7 0.2 %collective-permute-start.1 = (bf16[512,128]{1,0:T(8,128)(2,1)S(1)}, bf16[512,128]{1,0:T(8,128)(2,1)S(1)}, u32[]{:S(2)}, u32[]{:S(2)}) collective-permute-start(bf16[512,128]{1,0:T(8,128)(2,1)S(1)} %get-tuple-element.12.refs_0_), channel_id=1, source_target_pairs={{0,2},{1,3},{2,0},{3,1},{4,6},{5,7},{6,4},{7,5},{8,10},{9,11},{10,... | collective-permute-start | bytes 393224 | tf_op jit(solution)/shard_map/ppermute | solution.py:200
  9.9 0.3 %collective-permute-done.4.refs_4_ = bf16[256,768]{1,0:T(8,128)(2,1)S(1)} collective-permute-done((bf16[256,768]{1,0:T(8,128)(2,1)S(1)}, bf16[256,768]{1,0:T(8,128)(2,1)S(1)}, u32[]{:S(2)}, u32[]{:S(2)}) %collective-permute-start.4) | collective-permute-done | bytes 393248 | tf_op jit(solution)/shard_map/ppermute | solution.py:210
  10.2 3.5 %collective-permute-start.7 = (bf16[256,768]{1,0:T(8,128)(2,1)S(1)}, bf16[256,768]{1,0:T(8,128)(2,1)S(1)}, u32[]{:S(2)}, u32[]{:S(2)}) collective-permute-start(bf16[256,768]{1,0:T(8,128)(2,1)S(1)} %collective-permute-done.4.refs_4_), channel_id=1, source_target_pairs={{0,16},{1,9},{2,18},{3,11},{4,20},{5,13},{6,22},{7,15},{8,24},{9,1... | collective-permute-start | bytes 1179656 | tf_op jit(solution)/shard_map/ppermute | solution.py:210
  13.7 3.2 %collective-permute-done.refs_1_ = bf16[512,128]{1,0:T(8,128)(2,1)S(1)} collective-permute-done((bf16[512,128]{1,0:T(8,128)(2,1)S(1)}, bf16[512,128]{1,0:T(8,128)(2,1)S(1)}, u32[]{:S(2)}, u32[]{:S(2)}) %collective-permute-start) | collective-permute-done | bytes 131104 | tf_op jit(solution)/shard_map/ppermute | solution.py:200
  17.0 0.1 collective-permute-start.3
  17.1 0.0 collective-permute-done.2.block_ref
  17.1 1.0 %collective-permute-done.1.refs_0_ = bf16[512,128]{1,0:T(8,128)(2,1)S(1)} collective-permute-done((bf16[512,128]{1,0:T(8,128)(2,1)S(1)}, bf16[512,128]{1,0:T(8,128)(2,1)S(1)}, u32[]{:S(2)}, u32[]{:S(2)}) %collective-permute-start.1) | collective-permute-done | bytes 131104 | tf_op jit(solution)/shard_map/ppermute | solution.py:200
  18.1 0.1 collective-permute-start.6
  18.2 0.0 copy-done.1
  18.2 0.1 copy.9.row_ids_ref
  18.3 0.3 %collective-permute-done.3.refs_2_ = bf16[512,256]{1,0:T(8,128)(2,1)S(1)} collective-permute-done((bf16[512,256]{1,0:T(8,128)(2,1)S(1)}, bf16[512,256]{1,0:T(8,128)(2,1)S(1)}, u32[]{:S(2)}, u32[]{:S(2)}) %collective-permute-start.3) | collective-permute-done | bytes 262176 | tf_op jit(solution)/shard_map/ppermute | solution.py:200
  18.6 0.0 collective-permute-done.5.refs_5_
  18.6 0.0 copy-done
  18.6 1.2 %shard_map.68 = (f32[512,768]{1,0:T(8,128)S(1)}, bf16[512,256]{1,0:T(8,128)(2,1)S(1)}, f32[8,768]{1,0:T(8,128)S(1)}, bf16[512,768]{1,0:T(8,128)(2,1)S(1)}) custom-call(s32[8,1]{1,0:T(8,128)S(1)} %copy.9.row_ids_ref, s32[12,32]{1,0:T(8,128)S(1)} %bitcast.3, bf16[512,256]{1,0:T(8,128)(2,1)S(1)} %shard_map.65.refs_0_, bf16[512,256]{1,0:T(8,128)(2,1)S(1)} %shard_map.67.refs_1_, ...), custom_call_target="tpu_custom_call" | custom-call | flops 301989888 | bytes 1572864 | tf_op jit(solution)/shard_map/pallas_call | solution.py:121
  19.8 0.0 collective-permute-done.6.a_ref
  19.8 0.3 %collective-permute-done.7.b_ref = bf16[256,768]{1,0:T(8,128)(2,1)S(1)} collective-permute-done((bf16[256,768]{1,0:T(8,128)(2,1)S(1)}, bf16[256,768]{1,0:T(8,128)(2,1)S(1)}, u32[]{:S(2)}, u32[]{:S(2)}) %collective-permute-start.7) | collective-permute-done | bytes 393248 | tf_op jit(solution)/shard_map/ppermute | solution.py:210
  20.2 1.4 %shard_map.69 = (bf16[512,768]{1,0:T(8,128)(2,1)}, bf16[512,768]{1,0:T(8,128)(2,1)S(1)}) custom-call(f32[8,768]{1,0:T(8,128)S(1)} %get-tuple-element.14.keep_ref, f32[512,768]{1,0:T(8,128)S(1)} %get-tuple-element.15.total_ref, bf16[512,256]{1,0:T(8,128)(2,1)S(1)} %get-tuple-element.16.tail_ref, ...), custom_call_target="tpu_custom_call", output_to_operand_aliasing={{1}: (5, {})} | custom-call | flops 402653184 | bytes 2359296 | tf_op jit(solution)/shard_map/pallas_call | solution.py:181
  (3 shorter events, 0.1 us)
Async XLA Ops:
  0.0 18.2 %copy-start.1 = (s32[8]{0:T(128)S(1)}, s32[8]{0:T(128)}, u32[]{:S(2)}) copy-start(s32[8]{0:T(128)} %param.6) | copy-start | bytes 100
  0.0 18.6 %copy-start = (s32[32,12]{0,1:T(8,128)S(1)}, s32[32,12]{0,1:T(8,128)}, u32[]{:S(2)}) copy-start(s32[32,12]{0,1:T(8,128)} %param.11) | copy-start | bytes 4612
  1.2 9.0 %collective-permute-start.4 = (bf16[256,768]{1,0:T(8,128)(2,1)S(1)}, bf16[256,768]{1,0:T(8,128)(2,1)S(1)}, u32[]{:S(2)}, u32[]{:S(2)}) collective-permute-start(bf16[256,768]{1,0:T(8,128)(2,1)S(1)} %get-tuple-element.13.refs_3_), channel_id=1, source_target_pairs={{0,8},{1,17},{2,10},{3,19},{4,12},{5,21},{6,14},{7,23},{8,0},{9,25... | collective-permute-start | bytes 1179656 | tf_op jit(solution)/shard_map/ppermute | solution.py:210
  4.2 12.7 %collective-permute-start = (bf16[512,128]{1,0:T(8,128)(2,1)S(1)}, bf16[512,128]{1,0:T(8,128)(2,1)S(1)}, u32[]{:S(2)}, u32[]{:S(2)}) collective-permute-start(bf16[512,128]{1,0:T(8,128)(2,1)S(1)} %get-tuple-element.12.refs_0_), channel_id=1, source_target_pairs={{0,4},{1,5},{2,6},{3,7},{4,0},{5,1},{6,2},{7,3},{8,12},{9,13},{10,... | collective-permute-start | bytes 393224 | tf_op jit(solution)/shard_map/ppermute | solution.py:200
  6.8 10.2 %collective-permute-start.2 = (bf16[512,128]{1,0:T(8,128)(2,1)S(1)}, bf16[512,128]{1,0:T(8,128)(2,1)S(1)}, u32[]{:S(2)}, u32[]{:S(2)}) collective-permute-start(bf16[512,128]{1,0:T(8,128)(2,1)S(1)} %get-tuple-element.12.refs_0_), channel_id=1, source_target_pairs={{0,6},{1,7},{2,4},{3,5},{4,2},{5,3},{6,0},{7,1},{8,14},{9,15},{10,... | collective-permute-start | bytes 393224 | tf_op jit(solution)/shard_map/ppermute | solution.py:200
  8.2 10.4 %collective-permute-start.5 = (bf16[256,768]{1,0:T(8,128)(2,1)S(1)}, bf16[256,768]{1,0:T(8,128)(2,1)S(1)}, u32[]{:S(2)}, u32[]{:S(2)}) collective-permute-start(bf16[256,768]{1,0:T(8,128)(2,1)S(1)} %get-tuple-element.13.refs_3_), channel_id=1, source_target_pairs={{0,16},{1,9},{2,18},{3,11},{4,20},{5,13},{6,22},{7,15},{8,24},{9,1... | collective-permute-start | bytes 1179656 | tf_op jit(solution)/shard_map/ppermute | solution.py:210
  9.7 8.4 %collective-permute-start.1 = (bf16[512,128]{1,0:T(8,128)(2,1)S(1)}, bf16[512,128]{1,0:T(8,128)(2,1)S(1)}, u32[]{:S(2)}, u32[]{:S(2)}) collective-permute-start(bf16[512,128]{1,0:T(8,128)(2,1)S(1)} %get-tuple-element.12.refs_0_), channel_id=1, source_target_pairs={{0,2},{1,3},{2,0},{3,1},{4,6},{5,7},{6,4},{7,5},{8,10},{9,11},{10,... | collective-permute-start | bytes 393224 | tf_op jit(solution)/shard_map/ppermute | solution.py:200
  10.2 10.0 %collective-permute-start.7 = (bf16[256,768]{1,0:T(8,128)(2,1)S(1)}, bf16[256,768]{1,0:T(8,128)(2,1)S(1)}, u32[]{:S(2)}, u32[]{:S(2)}) collective-permute-start(bf16[256,768]{1,0:T(8,128)(2,1)S(1)} %collective-permute-done.4.refs_4_), channel_id=1, source_target_pairs={{0,16},{1,9},{2,18},{3,11},{4,20},{5,13},{6,22},{7,15},{8,24},{9,1... | collective-permute-start | bytes 1179656 | tf_op jit(solution)/shard_map/ppermute | solution.py:210
  17.0 1.6 %collective-permute-start.3 = (bf16[512,256]{1,0:T(8,128)(2,1)S(1)}, bf16[512,256]{1,0:T(8,128)(2,1)S(1)}, u32[]{:S(2)}, u32[]{:S(2)}) collective-permute-start(bf16[512,256]{1,0:T(8,128)(2,1)S(1)} %shard_map.65.refs_0_), channel_id=1, source_target_pairs={{0,1},{1,0},{2,3},{3,2},{4,5},{5,4},{6,7},{7,6},{8,9},{9,8},{10,11... | collective-permute-start | bytes 786440 | tf_op jit(solution)/shard_map/ppermute | solution.py:200
  18.1 1.7 %collective-permute-start.6 = (bf16[512,256]{1,0:T(8,128)(2,1)S(1)}, bf16[512,256]{1,0:T(8,128)(2,1)S(1)}, u32[]{:S(2)}, u32[]{:S(2)}) collective-permute-start(bf16[512,256]{1,0:T(8,128)(2,1)S(1)} %shard_map.67.refs_1_), channel_id=1, source_target_pairs={{0,1},{1,0},{2,3},{3,2},{4,5},{5,4},{6,7},{7,6},{8,9},{9,8},{10,11... | collective-permute-start | bytes 786440 | tf_op jit(solution)/shard_map/ppermute | solution.py:200
